TPU v7x, 256 devices: a whole 4x4x8 slice. The times are simulated.
256 devices in a mesh: row: 32 (over z, y_hi, core), col: 8 (over y_lo, x).
Axes of the slice: x: 4, y: 4 (y_hi: 2, y_lo: 2; y = y_hi * 2 + y_lo), z: 8, core: 2. Of those that a mesh axis runs over, the one named last changes fastest.
Arguments:
- img_emb: bfloat16 [131072, 1152], P(('row', 'col')), may hold values from -0.1796875 to 0.1796875
- txt_feat: bfloat16 [131072, 1152], P(('row', 'col')), may hold values from -6 to 6
- head_weight: bfloat16 [1152, 1152], replicated, may hold values from -0.1875 to 0.1875
- positive: int32 [256, 512], P(('row', 'col')), may hold values from 0 to 511, each once within a row
Outputs:
- img_grad: bfloat16 [131072, 1152], P(('row', 'col'))
- txt_grad: bfloat16 [131072, 1152], P(('row', 'col'))
- head_grad: float32 [1152, 1152], P('row', 'col')
Inputs may be any that keep to these rules, and one draw needn't show every extreme that they name: Each row of positive is a permutation of the rows of one device.
All inputs are finite; a program needn't handle non-finite values.
Results may differ from a plain program's by a relative error of at most 0.015.
Values may be sent and summed in bfloat16 or wider, within the bound.
No kernel may reach another device: no remote copies, remote signals or barrier semaphores. Data moves between devices by JAX's collectives and lax.ppermute only.
A program may use at most 64 MiB of HBM per device.

v0:
```python
import jax
import jax.numpy as jnp
from jax import lax
from jax.sharding import PartitionSpec as P

scale_logit = 8.0
bias_logit = -2.0


def from_partner(block, axis, apart):
    count = lax.axis_size(axis)
    route = []
    for low in range(count):
        high = low | 1 << apart
        if high != low and high < count:
            route += [(low, high), (high, low)]
    return lax.ppermute(block, axis, route)


def block_terms(zi, zt, labels):
    logits = (
        scale_logit
        * lax.dot_general(zi, zt, (((1,), (1,)), ((), ())), preferred_element_type=jnp.float32)
        + bias_logit
    )
    sign = jnp.where(labels, 1.0, -1.0).astype(jnp.float32)
    dsc = (-scale_logit * sign * jax.nn.sigmoid(-sign * logits)).astype(jnp.bfloat16)
    to_img = jnp.dot(dsc, zt, preferred_element_type=jnp.float32)
    to_txt = lax.dot_general(dsc, zi, (((0,), (0,)), ((), ())), preferred_element_type=jnp.float32)
    return (to_img, to_txt)


def shards(img_emb, txt_feat, head_weight, positive):
    rows_here = img_emb.shape[0]
    width = img_emb.shape[1]
    row_count = lax.axis_size("row")
    col_count = lax.axis_size("col")
    devices = row_count * col_count
    row_bit = row_count.bit_length() - 2
    col_bit = col_count.bit_length() - 2
    u = jnp.dot(txt_feat, head_weight, preferred_element_type=jnp.float32)
    tnorm = jnp.sqrt(jnp.sum(u * u, axis=-1, keepdims=True) + 1e-06)
    that = u / tnorm
    zt = that.astype(jnp.bfloat16)
    imgf = img_emb.astype(jnp.float32)
    inorm = jnp.sqrt(jnp.sum(imgf * imgf, axis=-1, keepdims=True) + 1e-06)
    ihat = imgf / inorm
    zi = ihat.astype(jnp.bfloat16)
    partner_one = from_partner(zt, "row", row_bit)
    partner_two = from_partner(zt, "col", col_bit)
    columns = jnp.arange(rows_here, dtype=jnp.int32)
    labels = positive[0][:, None] == columns[None, :]
    none = jnp.zeros((rows_here, rows_here), dtype=bool)
    img_own, txt_own = block_terms(zi, zt, labels)
    img_one, txt_one = block_terms(zi, partner_one, none)
    img_two, txt_two = block_terms(zi, partner_two, none)
    back_one = from_partner(txt_one.astype(jnp.bfloat16), "row", row_bit)
    back_two = from_partner(txt_two.astype(jnp.bfloat16), "col", col_bit)
    dzi = img_own + img_one + img_two
    dzt = txt_own + back_one.astype(jnp.float32) + back_two.astype(jnp.float32)
    img_grad = ((dzi - ihat * jnp.sum(ihat * dzi, axis=-1, keepdims=True)) / inorm).astype(
        jnp.bfloat16
    )
    du = ((dzt - that * jnp.sum(that * dzt, axis=-1, keepdims=True)) / tnorm).astype(jnp.bfloat16)
    txt_grad = lax.dot_general(
        du, head_weight, (((1,), (1,)), ((), ())), preferred_element_type=jnp.float32
    ).astype(jnp.bfloat16)
    share_rows = width // row_count
    share_cols = width // col_count
    local_head = lax.dot_general(
        txt_feat, du, (((0,), (0,)), ((), ())), preferred_element_type=jnp.float32
    )
    summed = lax.psum(local_head, ("row", "col"))
    start_row = lax.axis_index("row") * share_rows
    start_col = lax.axis_index("col") * share_cols
    head_share = lax.dynamic_slice(summed, (start_row, start_col), (share_rows, share_cols))
    head_grad = head_share / devices
    return (img_grad, txt_grad, head_grad)


def solution(mesh):
    return jax.shard_map(
        shards,
        mesh=mesh,
        in_specs=(P(("row", "col"), None), P(("row", "col"), None), P(), P(("row", "col"), None)),
        out_specs=(P(("row", "col"), None), P(("row", "col"), None), P("row", "col")),
        check_vma=False,
    )
```

profile of v0, /device:TPU:32, one launch (start us, length us, event | category | flops | bytes accessed | tf_op | source)
XLA Modules:
  0.0 417.9 jit_solution(9098860698768139018)
XLA Ops:
  7.2 1.7 copy-done
  8.9 3.2 multiply_reduce_fusion.2
  12.2 0.2 fusion.24
  12.4 1.1 copy-done.3
  13.6 1.6 collective-permute-start.1
  15.1 6.3 %collective-permute-start = (bf16[512,1152]{1,0:T(8,128)(2,1)S(1)}, bf16[512,1152]{1,0:T(8,128)(2,1)S(1)}, u32[]{:S(2)}, u32[]{:S(2)}) collective-permute-start(bf16[512,1152]{1,0:T(8,128)(2,1)S(1)} %fusion.24), channel_id=1, source_target_pairs={{0,128},{128,0},{8,136},{136,8},{16,144},{144,16},{24,152},{152,24... | collective-permute-start | bytes 3538952 | tf_op jit(solution)/shard_map/ppermute | solution.py:17
  21.4 0.3 fusion
  21.7 0.4 fusion.23
  22.1 19.1 %collective-permute-done.1 = bf16[512,1152]{1,0:T(8,128)(2,1)S(1)} collective-permute-done((bf16[512,1152]{1,0:T(8,128)(2,1)S(1)}, bf16[512,1152]{1,0:T(8,128)(2,1)S(1)}, u32[]{:S(2)}, u32[]{:S(2)}) %collective-permute-start.1) | collective-permute-done | bytes 1179680 | tf_op jit(solution)/shard_map/ppermute | solution.py:17
  41.3 1.0 fusion.21
  42.3 1.9 convolution_convert_fusion.1
  44.2 1.6 collective-permute-start.3
  45.8 26.9 %collective-permute-done = bf16[512,1152]{1,0:T(8,128)(2,1)S(1)} collective-permute-done((bf16[512,1152]{1,0:T(8,128)(2,1)S(1)}, bf16[512,1152]{1,0:T(8,128)(2,1)S(1)}, u32[]{:S(2)}, u32[]{:S(2)}) %collective-permute-start) | collective-permute-done | bytes 1179680 | tf_op jit(solution)/shard_map/ppermute | solution.py:17
  72.7 1.0 fusion.22
  73.8 1.9 convolution_convert_fusion.2
  75.7 5.5 %collective-permute-start.2 = (bf16[512,1152]{1,0:T(8,128)(2,1)}, bf16[512,1152]{1,0:T(8,128)(2,1)}, u32[]{:S(2)}, u32[]{:S(2)}) collective-permute-start(bf16[512,1152]{1,0:T(8,128)(2,1)} %convolution_convert_fusion.2), channel_id=1, source_target_pairs={{0,128},{128,0},{8,136},{136,8},{16,144},{144,16},{24,152},{152,24... | collective-permute-start | bytes 3538952 | tf_op jit(solution)/shard_map/ppermute | solution.py:17
  81.2 2.9 fusion.20
  84.2 44.0 %collective-permute-done.2 = bf16[512,1152]{1,0:T(8,128)(2,1)} collective-permute-done((bf16[512,1152]{1,0:T(8,128)(2,1)}, bf16[512,1152]{1,0:T(8,128)(2,1)}, u32[]{:S(2)}, u32[]{:S(2)}) %collective-permute-start.2) | collective-permute-done | bytes 1179680 | tf_op jit(solution)/shard_map/ppermute | solution.py:17
  128.2 3.0 multiply_reduce_fusion
  131.2 2.5 divide_convert_fusion
  133.7 1.0 copy-done.5
  134.7 4.1 convolution_bitcast_fusion
  138.9 2.2 fusion.25
  141.2 0.9 convolution_add_fusion.1
  142.1 0.4 copy-done.2
  142.4 0.4 copy-done.16
  142.9 1.1 multiply_reduce_fusion.1
  144.0 1.5 divide_convert_fusion.1
  145.5 2.9 convolution_convert_fusion
  148.4 260.9 %all-reduce.2.cloned.1.call-done = f32[1152,1152]{0,1:T(8,128)} async-done(((f32[1152,1152]{0,1:T(8,128)}), f32[1152,1152]{0,1:T(8,128)}) %all-reduce.2.cloned.1.call-update) | async-done | bytes 5308432 | tf_op jit(solution)/shard_map/psum | solution.py:73
  409.4 1.0 dynamic-slice_multiply_fusion
  410.4 0.7 copy.7
  (40 shorter events, 0.3 us)
Async XLA Ops:
  7.2 1.8 copy-start
  7.2 402.2 %all-reduce.2.cloned.1.call-start = ((), (), s32[]{:S(2)}) async-start(), calls=%async_computation | async-start | bytes 10616832 | tf_op jit(solution)/shard_map/psum | solution.py:73
  12.1 1.4 copy-start.3
  12.1 9.3 %copy-start.1 = (bf16[512,1152]{1,0:T(8,128)(2,1)S(1)}, bf16[512,1152]{1,0:T(8,128)(2,1)}, u32[]{:S(2)}) copy-start(bf16[512,1152]{1,0:T(8,128)(2,1)} %param.4) | copy-start | bytes 3538948
  13.6 8.6 %copy-start.7 = (bf16[512,1152]{1,0:T(8,128)(2,1)}, bf16[512,1152]{1,0:T(8,128)(2,1)S(1)}, u32[]{:S(2)}) copy-start(bf16[512,1152]{1,0:T(8,128)(2,1)S(1)} %fusion.24) | copy-start | bytes 3538948
  13.6 27.7 %collective-permute-start.1 = (bf16[512,1152]{1,0:T(8,128)(2,1)S(1)}, bf16[512,1152]{1,0:T(8,128)(2,1)S(1)}, u32[]{:S(2)}, u32[]{:S(2)}) collective-permute-start(bf16[512,1152]{1,0:T(8,128)(2,1)S(1)} %fusion.24), channel_id=1, source_target_pairs={{0,4},{4,0},{1,5},{5,1},{2,6},{6,2},{3,7},{7,3},{8,12},{12,8},{9,1... | collective-permute-start | bytes 3538952 | tf_op jit(solution)/shard_map/ppermute | solution.py:17
  15.1 57.6 %collective-permute-start = (bf16[512,1152]{1,0:T(8,128)(2,1)S(1)}, bf16[512,1152]{1,0:T(8,128)(2,1)S(1)}, u32[]{:S(2)}, u32[]{:S(2)}) collective-permute-start(bf16[512,1152]{1,0:T(8,128)(2,1)S(1)} %fusion.24), channel_id=1, source_target_pairs={{0,128},{128,0},{8,136},{136,8},{16,144},{144,16},{24,152},{152,24... | collective-permute-start | bytes 3538952 | tf_op jit(solution)/shard_map/ppermute | solution.py:17
  22.1 51.6 %copy-start.8 = (bf16[512,1152]{1,0:T(8,128)(2,1)}, bf16[512,1152]{1,0:T(8,128)(2,1)S(1)}, u32[]{:S(2)}) copy-start(bf16[512,1152]{1,0:T(8,128)(2,1)S(1)} %fusion.23) | copy-start | bytes 3538948
  41.3 1.0 copy-start.15
  42.3 1.9 copy-start.18
  44.2 40.0 %collective-permute-start.3 = (bf16[512,1152]{1,0:T(8,128)(2,1)}, bf16[512,1152]{1,0:T(8,128)(2,1)}, u32[]{:S(2)}, u32[]{:S(2)}) collective-permute-start(bf16[512,1152]{1,0:T(8,128)(2,1)} %convolution_convert_fusion.1), channel_id=1, source_target_pairs={{0,4},{4,0},{1,5},{5,1},{2,6},{6,2},{3,7},{7,3},{8,12},{12,8},{9,1... | collective-permute-start | bytes 3538952 | tf_op jit(solution)/shard_map/ppermute | solution.py:17
  72.7 1.1 copy-start.11
  73.8 1.9 copy-start.13
  73.8 7.5 %copy-start.17 = (s32[1,512]{1,0:T(1,128)S(1)}, s32[1,512]{1,0:T(1,128)}, u32[]{:S(2)}) copy-start(s32[1,512]{1,0:T(1,128)} %param.7) | copy-start | bytes 6148
  75.7 52.5 %collective-permute-start.2 = (bf16[512,1152]{1,0:T(8,128)(2,1)}, bf16[512,1152]{1,0:T(8,128)(2,1)}, u32[]{:S(2)}, u32[]{:S(2)}) collective-permute-start(bf16[512,1152]{1,0:T(8,128)(2,1)} %convolution_convert_fusion.2), channel_id=1, source_target_pairs={{0,128},{128,0},{8,136},{136,8},{16,144},{144,16},{24,152},{152,24... | collective-permute-start | bytes 3538952 | tf_op jit(solution)/shard_map/ppermute | solution.py:17
  81.2 47.0 %copy-start.4 = (f32[512,1152]{1,0:T(8,128)S(1)}, f32[512,1152]{1,0:T(8,128)}, u32[]{:S(2)}) copy-start(f32[512,1152]{1,0:T(8,128)} %copy-done.3) | copy-start | bytes 7077892
  81.2 47.0 %copy-start.9 = (bf16[512,1152]{1,0:T(8,128)(2,1)S(1)}, bf16[512,1152]{1,0:T(8,128)(2,1)}, u32[]{:S(2)}) copy-start(bf16[512,1152]{1,0:T(8,128)(2,1)} %copy-done.8) | copy-start | bytes 3538948
  131.2 3.5 copy-start.10
  133.7 1.0 copy-start.5
  138.9 2.3 copy-start.12
  138.9 2.3 copy-start.14
  141.1 1.3 copy-start.2
  141.2 1.6 copy-start.16
  141.2 1.7 copy-start.19
  144.0 1.5 copy-start.6
Sparse Core Ops, SparseCore 0:
  139.0 270.3 all-reduce.1
where the time goes:
time: 421 us; the launch traced here: 418 us
  waiting for transfers between devices  351 us (83%)
  matrix products  26.2 us (6%)
  starting transfers between devices  15 us (4%)
  between operations  14.3 us (3%)
  other arithmetic  5.93 us (1%)
  local copies, waits for them, and re-layouts  5.5 us (1%)
    psum x1, waiting for transfers between devices, shards(): summed = lax.psum(local_head, ('row', 'col'))  261 us
    ppermute x4, waiting for transfers between devices, from_partner(): return lax.ppermute(block, axis, route)  90 us
    ppermute x4, starting transfers between devices, from_partner(): return lax.ppermute(block, axis, route)  15 us
  transfers between devices with their start and end apart: 5, of which 4 were waited for; matrix products, arithmetic and copies ran while one was open for 4% of the time, Pallas kernels for 0%

commit v1 on v0

v1 whole, which is shorter than its diff:
```python
import jax
import jax.numpy as jnp
from jax import lax
from jax.sharding import PartitionSpec as P

scale_logit = 8.0
bias_logit = -2.0
f32 = jnp.float32
bf16 = jnp.bfloat16


def from_partner(block, axis, mask):
    count = lax.axis_size(axis)
    return lax.ppermute(block, axis, [(low, low ^ mask) for low in range(count)])


def rows_by_rows(a, b):
    return lax.dot_general(a, b, (((1,), (1,)), ((), ())), preferred_element_type=f32)


def columns_by_columns(a, b):
    return lax.dot_general(a, b, (((0,), (0,)), ((), ())), preferred_element_type=f32)


def unit(img):
    wide = img.astype(f32)
    norm = jnp.sqrt(jnp.sum(wide * wide, axis=-1, keepdims=True) + 1e-06)
    hat = wide / norm
    return hat, norm, hat.astype(bf16)


def unpaired(zi, zt):
    logits = scale_logit * rows_by_rows(zi, zt) + bias_logit
    return (scale_logit * jax.nn.sigmoid(logits)).astype(bf16)


def paired(zi, zt, labels):
    logits = scale_logit * rows_by_rows(zi, zt) + bias_logit
    sign = jnp.where(labels, 1.0, -1.0).astype(f32)
    return (-scale_logit * sign * jax.nn.sigmoid(-sign * logits)).astype(bf16)


def shards(img_emb, txt_feat, head_weight, positive):
    rows, width = img_emb.shape
    n_row = lax.axis_size("row")
    n_col = lax.axis_size("col")
    row_mask = n_row // 2
    col_mask = n_col // 2
    share_rows = width // n_row
    share_cols = width // n_col
    half = rows // 2
    parts = [slice(0, half), slice(half, rows)]

    img_two = from_partner(img_emb, "col", col_mask)
    img_one = [from_partner(img_emb[p], "row", row_mask) for p in parts]

    u = jnp.dot(txt_feat, head_weight, preferred_element_type=f32)
    tnorm = jnp.sqrt(jnp.sum(u * u, axis=-1, keepdims=True) + 1e-06)
    that = u / tnorm
    zt = that.astype(bf16)
    txt_two = from_partner(zt, "col", col_mask)
    txt_one = [from_partner(zt[p], "row", row_mask) for p in parts]

    core = lax.axis_index("row") & 1
    lane = jnp.arange(width // 2, dtype=jnp.int32)
    place = lane // share_rows
    depth = n_row // 4
    block = (place % depth) * 4 + (place // depth) * 2
    source = block * share_rows + lane % share_rows
    column = jnp.arange(width, dtype=jnp.int32)[:, None]

    def pick(which):
        choose = (column == (source + which * share_rows)[None, :]).astype(bf16)
        return jnp.dot(txt_feat, choose, preferred_element_type=f32).astype(bf16)

    txt_mine = pick(core)
    txt_theirs = pick(1 - core)

    ihat, inorm, zi = unit(img_emb)
    columns = jnp.arange(rows, dtype=jnp.int32)
    labels = positive[0][:, None] == columns[None, :]
    dsc = paired(zi, zt, labels)
    dzi = jnp.dot(dsc, zt, preferred_element_type=f32)
    dzt = columns_by_columns(dsc, zi)

    for img in [img_two] + img_one:
        zi_from = unit(img)[2]
        dzt = dzt + columns_by_columns(unpaired(zi_from, zt), zi_from)

    du = ((dzt - that * jnp.sum(that * dzt, axis=-1, keepdims=True)) / tnorm).astype(bf16)
    head_theirs = columns_by_columns(du, txt_theirs).astype(bf16)
    head_theirs = from_partner(head_theirs, "row", 1)
    head = columns_by_columns(du, txt_mine) + head_theirs.astype(f32)
    head = lax.all_to_all(head.astype(bf16), "col", 0, 0, tiled=True)
    head = jnp.sum(head.reshape(n_col, share_cols, width // 2).astype(f32), axis=0).astype(bf16)
    head = head.reshape(share_cols, n_row // 2, share_rows).transpose(1, 0, 2)
    groups = [[z * 4 + y * 2 + c for y in range(2) for z in range(depth)] for c in range(2)]
    head = lax.all_to_all(head, "row", 0, 0, axis_index_groups=groups, tiled=True)
    head = jnp.sum(head.astype(f32), axis=0).T
    head_grad = head / (n_row * n_col)

    txt_grad = rows_by_rows(du, head_weight).astype(bf16)

    for zt_from in [txt_two] + txt_one:
        dzi = dzi + jnp.dot(unpaired(zi, zt_from), zt_from, preferred_element_type=f32)
    img_grad = ((dzi - ihat * jnp.sum(ihat * dzi, axis=-1, keepdims=True)) / inorm).astype(bf16)
    return (img_grad, txt_grad, head_grad)


def solution(mesh):
    return jax.shard_map(
        shards,
        mesh=mesh,
        in_specs=(P(("row", "col"), None), P(("row", "col"), None), P(), P(("row", "col"), None)),
        out_specs=(P(("row", "col"), None), P(("row", "col"), None), P("row", "col")),
        check_vma=False,
    )
```

time: 421 us -> 186 us (0.44)
  waiting for transfers between devices: 351 us -> 50 us
  starting transfers between devices: 15 us -> 51.3 us
  matrix products: 26.2 us -> 59.1 us
  between operations: 14.3 us -> 0.73 us
  other arithmetic: 5.93 us -> 15.6 us
    psum x1 -> x0, waiting for transfers between devices: 261 us -> none  [shards(): summed = lax.psum(local_head, ('row', 'col'))]
    ppermute x4 -> x7, waiting for transfers between devices: 90 us -> 30.5 us  [from_partner(): lax.ppermute(block, axis, [(low, low ^ mask) for low in range(count)])]
    dot_general x12 -> x13, matrix products: 26.2 us -> 59.1 us  [the longest x6 30.1 us: columns_by_columns(): lax.dot_general(a, b, (((0,), (0,)), ((), ())), preferred_element_type=f32)]
    all_to_all x0 -> x2, starting transfers between devices: none -> 30.8 us  [the longest x1 26.3 us: shards(): lax.all_to_all(head, 'row', 0, 0, axis_index_groups=groups, tiled=True)]
    all_to_all x0 -> x2, waiting for transfers between devices: none -> 19.5 us  [the longest x1 11.1 us: shards(): head = lax.all_to_all(head.astype(bf16), 'col', 0, 0, tiled=True)]
    reduce_sum x1 -> x6, other arithmetic: 0.3 us -> 6.08 us  [the longest x4 4.4 us: unit(): norm = jnp.sqrt(jnp.sum(wide * wide, axis=-1, keepdims=True) + 1e-06)]
    ppermute x4 -> x7, starting transfers between devices: 15 us -> 20.4 us  [from_partner(): lax.ppermute(block, axis, [(low, low ^ mask) for low in range(count)])]
    unnamed x41 -> x10, local copies, waits for them, and re-layouts: 5.5 us -> 0.24 us
  transfers between devices with their start and end apart: 5 -> 9, of which waited for: 4 -> 4; matrix products, arithmetic and copies ran while one was open for 4% -> 43% of each run, Pallas kernels for 0% -> 0%
where the time goes in v1:
time: 186 us; the launch traced here: 185 us
  matrix products  59.1 us (32%)
  starting transfers between devices  51.3 us (28%)
  waiting for transfers between devices  50 us (27%)
  other arithmetic  15.6 us (8%)
  local copies, waits for them, and re-layouts  8.56 us (5%)
    ppermute x7, waiting for transfers between devices, from_partner(): lax.ppermute(block, axis, [(low, low ^ mask) for low in range(count)])  30.5 us
    dot_general x6, matrix products, columns_by_columns(): lax.dot_general(a, b, (((0,), (0,)), ((), ())), preferred_element_type=f32)  30.1 us
    all_to_all x1, starting transfers between devices, shards(): lax.all_to_all(head, 'row', 0, 0, axis_index_groups=groups, tiled=True)  26.3 us
    ppermute x7, starting transfers between devices, from_partner(): lax.ppermute(block, axis, [(low, low ^ mask) for low in range(count)])  20.4 us
    dot_general x3, matrix products, shards(): jnp.dot(unpaired(zi, zt_from), zt_from, preferred_element_type=f32)  16.9 us
    all_to_all x1, waiting for transfers between devices, shards(): head = lax.all_to_all(head.astype(bf16), 'col', 0, 0, tiled=True)  11.1 us
    all_to_all x1, waiting for transfers between devices, shards(): lax.all_to_all(head, 'row', 0, 0, axis_index_groups=groups, tiled=True)  8.43 us
    dot_general x2, matrix products, rows_by_rows(): lax.dot_general(a, b, (((1,), (1,)), ((), ())), preferred_element_type=f32)  6.63 us
  transfers between devices with their start and end apart: 9, of which 4 were waited for; matrix products, arithmetic and copies ran while one was open for 43% of the time, Pallas kernels for 0%

profile of v1, /device:TPU:32, one launch (start us, length us, event | category | flops | bytes accessed | tf_op | source)
XLA Modules:
  0.0 185.3 jit_solution(3585250296707692525)
XLA Ops:
  0.7 1.7 collective-permute-start.3
  2.3 2.4 %fusion.155 = (bf16[256,1152]{1,0:T(8,128)(2,1)}, bf16[256,1152]{1,0:T(8,128)(2,1)}) fusion(bf16[512,1152]{1,0:T(8,128)(2,1)} %param.4), kind=kLoop, calls=%fused_computation.179 | loop fusion | bytes 2359296 | tf_op jit(solution)/shard_map/slice | solution.py:55
  4.7 6.3 %collective-permute-start.5 = (bf16[256,1152]{1,0:T(8,128)(2,1)}, bf16[256,1152]{1,0:T(8,128)(2,1)}, u32[]{:S(2)}, u32[]{:S(2)}) collective-permute-start(bf16[256,1152]{1,0:T(8,128)(2,1)} %get-tuple-element.4), channel_id=1, source_target_pairs={{0,128},{8,136},{16,144},{24,152},{32,160},{40,168},{48,176},{56,1... | collective-permute-start | bytes 1769480 | tf_op jit(solution)/shard_map/ppermute | solution.py:14
  11.0 1.9 %multiply_reduce_fusion.2 = (f32[512]{0:T(512)S(1)}, f32[512,1152]{1,0:T(8,128)S(1)}) fusion(bf16[512,1152]{1,0:T(8,128)(2,1)S(1)} %copy-done.3, bf16[1152,1152]{1,0:T(8,128)(2,1)S(1)} %copy-done), kind=kOutput, calls=%fused_computation.24 | convolution fusion | flops 1360133632 | bytes 6195200 | tf_op jit(solution)/shard_map/dot_general | solution.py:57
  13.0 1.5 fusion.145
  15.4 2.4 %fusion.156 = (bf16[256,1152]{1,0:T(8,128)(2,1)}, bf16[256,1152]{1,0:T(8,128)(2,1)}) fusion(bf16[512,1152]{1,0:T(8,128)(2,1)} %fusion.145), kind=kLoop, calls=%fused_computation.180 | loop fusion | bytes 2359296 | tf_op jit(solution)/shard_map/slice | solution.py:62
  17.8 5.9 %collective-permute-start.2 = (bf16[256,1152]{1,0:T(8,128)(2,1)}, bf16[256,1152]{1,0:T(8,128)(2,1)}, u32[]{:S(2)}, u32[]{:S(2)}) collective-permute-start(bf16[256,1152]{1,0:T(8,128)(2,1)} %get-tuple-element.6), channel_id=1, source_target_pairs={{0,128},{8,136},{16,144},{24,152},{32,160},{40,168},{48,176},{56,1... | collective-permute-start | bytes 1769480 | tf_op jit(solution)/shard_map/ppermute | solution.py:14
  24.1 2.5 %fusion.38 = bf16[512,512]{1,0:T(8,128)(2,1)S(1)} fusion(bf16[512,1152]{1,0:T(8,128)(2,1)} %fusion.145, s32[512]{0:T(512)S(1)} %bitcast.29, f32[512]{0:T(512)S(1)} %add_sqrt_fusion.2, bf16[512,1152]{1,0:T(8,128)(2,1)S(1)} %copy-done.1), kind=kOutput, calls=%fused_computation.59 | convolution fusion | flops 608894976 | bytes 2887680 | tf_op jit(solution)/shard_map/dot_general | solution.py:18
  26.5 3.5 %fusion.161 = f32[512,1152]{1,0:T(8,128)} fusion(bf16[512,512]{1,0:T(8,128)(2,1)S(1)} %fusion.38, bf16[512,1152]{1,0:T(8,128)(2,1)} %fusion.145), kind=kOutput, calls=%fused_computation.181 | convolution fusion | flops 603979776 | bytes 4063232 | tf_op jit(solution)/shard_map/dot_general | solution.py:83
  30.1 3.7 %fusion.146 = f32[512,1152]{1,0:T(8,128)} fusion(bf16[512,512]{1,0:T(8,128)(2,1)S(1)} %fusion.38, f32[512]{0:T(512)S(1)} %add_sqrt_fusion.2, bf16[512,1152]{1,0:T(8,128)(2,1)} %param.4), kind=kOutput, calls=%fused_computation.178 | convolution fusion | flops 605749248 | bytes 4065280 | tf_op jit(solution)/shard_map/dot_general | solution.py:22
  33.8 10.2 %collective-permute-done.5 = bf16[256,1152]{1,0:T(8,128)(2,1)} collective-permute-done((bf16[256,1152]{1,0:T(8,128)(2,1)}, bf16[256,1152]{1,0:T(8,128)(2,1)}, u32[]{:S(2)}, u32[]{:S(2)}) %collective-permute-start.5) | collective-permute-done | bytes 589856 | tf_op jit(solution)/shard_map/ppermute | solution.py:14
  44.0 5.8 %collective-permute-start.1 = (bf16[256,1152]{1,0:T(8,128)(2,1)}, bf16[256,1152]{1,0:T(8,128)(2,1)}, u32[]{:S(2)}, u32[]{:S(2)}) collective-permute-start(bf16[256,1152]{1,0:T(8,128)(2,1)} %get-tuple-element.5), channel_id=1, source_target_pairs={{0,128},{8,136},{16,144},{24,152},{32,160},{40,168},{48,176},{56,1... | collective-permute-start | bytes 1769480 | tf_op jit(solution)/shard_map/ppermute | solution.py:14
  51.1 20.2 %collective-permute-done.4 = bf16[256,1152]{1,0:T(8,128)(2,1)} collective-permute-done((bf16[256,1152]{1,0:T(8,128)(2,1)}, bf16[256,1152]{1,0:T(8,128)(2,1)}, u32[]{:S(2)}, u32[]{:S(2)}) %collective-permute-start.4) | collective-permute-done | bytes 589856 | tf_op jit(solution)/shard_map/ppermute | solution.py:14
  71.3 1.3 fusion.69
  72.6 4.3 %fusion.74 = f32[512,1152]{1,0:T(8,128)} fusion(bf16[512,1152]{1,0:T(8,128)(2,1)} %fusion.145, bf16[256,1152]{1,0:T(8,128)(2,1)} %collective-permute-done.5, f32[256]{0:T(256)S(1)} %add_sqrt_fusion.3), kind=kOutput, calls=%fused_computation.100 | convolution fusion | flops 606666752 | bytes 4129792 | tf_op jit(solution)/shard_map/dot_general | solution.py:22
  76.9 1.6 fusion.5
  78.5 6.0 %convolution_add_fusion.1 = f32[512,1152]{1,0:T(8,128)} fusion(f32[512,1152]{1,0:T(8,128)} %fusion.146, bf16[512,1152]{1,0:T(8,128)(2,1)} %fusion.145, bf16[512,1152]{1,0:T(8,128)(2,1)} %collective-permute-done.3, f32[512]{0:T(512)S(1)} %add_sqrt_fusion), kind=kOutput, calls=%fused_computation.2 | convolution fusion | flops 1213923328 | bytes 7079936 | tf_op jit(solution)/shard_map/dot_general | solution.py:22
  84.5 6.6 %multiply_reduce_fusion = (f32[512]{0:T(512)S(1)}, f32[512,1152]{1,0:T(8,128)}) fusion(f32[512,1152]{1,0:T(8,128)} %copy-done.2, f32[512]{0:T(512)S(1)} %add_sqrt_fusion.1, f32[512,1152]{1,0:T(8,128)} %fusion.74, f32[512,1152]{1,0:T(8,128)} %convolution_add_fusion.1, bf16[256,1152]{1,0:T(8,128)(2,1)} %collective-permute-done.4, f32[256]{0:T(256)S(1)} %add_sqrt_fusion.4, ...), kind=kOutput, calls=%fused_computation.21 | convolution fusion | flops 609615360 | bytes 11211776 | tf_op jit(solution)/shard_map/dot_general | solution.py:22
  91.1 3.8 %divide_convert_fusion = bf16[512,1152]{1,0:T(8,128)(2,1)} fusion(f32[512,1152]{1,0:T(8,128)} %get-tuple-element.12, f32[512]{0:T(512)S(1)} %get-tuple-element.11, f32[512]{0:T(512)S(1)} %add_sqrt_fusion.1, f32[512,1152]{1,0:T(8,128)} %copy-done.2), kind=kLoop, calls=%fused_computation.20 | loop fusion | flops 2949120 | bytes 5902336 | tf_op jit(solution)/shard_map/convert_element_type | solution.py:90
  94.9 4.6 %convolution_convert_fusion = bf16[1152,576]{0,1:T(8,128)(2,1)} fusion(bf16[512,1152]{1,0:T(8,128)(2,1)} %divide_convert_fusion, bf16[512,1152]{1,0:T(8,128)(2,1)} %param.5, s32[576]{0:T(1024)S(1)} %broadcast_add_fusion), kind=kOutput, calls=%fused_computation.6 | convolution fusion | flops 1361240064 | bytes 3688704 | tf_op jit(solution)/shard_map/dot_general | solution.py:22
  99.5 4.5 %fusion.73 = f32[512,1152]{1,0:T(8,128)} fusion(bf16[256,1152]{1,0:T(8,128)(2,1)} %collective-permute-done.2, f32[512]{0:T(512)S(1)} %add_sqrt_fusion.2, bf16[512,1152]{1,0:T(8,128)(2,1)} %param.4), kind=kOutput, calls=%fused_computation.99 | convolution fusion | flops 606666752 | bytes 4130816 | tf_op jit(solution)/shard_map/dot_general | solution.py:105
  104.1 5.9 %convolution_add_fusion.3 = f32[512,1152]{1,0:T(8,128)} fusion(f32[512,1152]{1,0:T(8,128)} %fusion.161, bf16[512,1152]{1,0:T(8,128)(2,1)} %collective-permute-done, f32[512]{0:T(512)S(1)} %add_sqrt_fusion.2, bf16[512,1152]{1,0:T(8,128)(2,1)} %param.4), kind=kOutput, calls=%fused_computation.5 | convolution fusion | flops 1212153856 | bytes 7079936 | tf_op jit(solution)/shard_map/dot_general | solution.py:105
  110.0 5.0 %add_convert_fusion = bf16[1152,576]{0,1:T(8,128)(2,1)} fusion(bf16[1152,576]{0,1:T(8,128)(2,1)} %collective-permute-done.6, bf16[512,1152]{1,0:T(8,128)(2,1)} %divide_convert_fusion, bf16[512,1152]{1,0:T(8,128)(2,1)} %param.5, s32[576]{0:T(1024)S(1)} %broadcast_add_fusion.1), kind=kOutput, calls=%fused_computation.16 | convolution fusion | flops 1362567168 | bytes 5015808 | tf_op jit(solution)/shard_map/dot_general | solution.py:22
  115.0 2.6 %copy.8 = bf16[1152,576]{1,0:T(8,128)(2,1)} copy(bf16[1152,576]{0,1:T(8,128)(2,1)} %add_convert_fusion) | data formatting | bytes 2654208 | tf_op jit(solution)/shard_map/convert_element_type | solution.py:94
  117.6 4.5 %all-to-all-start = ((bf16[8,144,576]{2,1,0:T(8,128)(2,1)}), bf16[8,144,576]{2,1,0:T(8,128)(2,1)}, u32[]{:S(2)}, u32[]{:S(2)}) async-start(bf16[8,144,576]{2,1,0:T(8,128)(2,1)} %bitcast.28), calls=%async_computation | async-start | bytes 2949120 | tf_op jit(solution)/shard_map/all_to_all | solution.py:94
  122.1 6.4 %multiply_reduce_fusion.1 = (f32[512]{0:T(512)S(1)}, f32[512,1152]{1,0:T(8,128)}) fusion(f32[512]{0:T(512)S(1)} %add_sqrt_fusion.2, bf16[512,1152]{1,0:T(8,128)(2,1)} %param.4, f32[512,1152]{1,0:T(8,128)} %fusion.73, f32[512,1152]{1,0:T(8,128)} %convolution_add_fusion.3, bf16[256,1152]{1,0:T(8,128)(2,1)} %collective-permute-done.1), kind=kOutput, calls=%fused_computation.23 | convolution fusion | flops 610205184 | bytes 8851456 | tf_op jit(solution)/shard_map/dot_general | solution.py:105
  128.5 3.5 %divide_convert_fusion.1 = bf16[512,1152]{1,0:T(8,128)(2,1)} fusion(f32[512,1152]{1,0:T(8,128)} %get-tuple-element.10, f32[512]{0:T(512)S(1)} %get-tuple-element.9, f32[512]{0:T(512)S(1)} %add_sqrt_fusion.2, bf16[512,1152]{1,0:T(8,128)(2,1)} %param.4), kind=kLoop, calls=%fused_computation.22 | loop fusion | flops 3538944 | bytes 4722688 | tf_op jit(solution)/shard_map/convert_element_type | solution.py:106
  132.1 11.1 %all-to-all-done = bf16[8,144,576]{2,1,0:T(8,128)(2,1)} async-done(((bf16[8,144,576]{2,1,0:T(8,128)(2,1)}), bf16[8,144,576]{2,1,0:T(8,128)(2,1)}, u32[]{:S(2)}, u32[]{:S(2)}) %all-to-all-start) | async-done | bytes 1327136 | tf_op jit(solution)/shard_map/all_to_all | solution.py:94
  143.2 1.6 reduce_sum.91
  145.7 26.3 %all-to-all-start.1 = ((bf16[16,144,36]{1,2,0:T(8,128)(2,1)}), bf16[16,144,36]{1,2,0:T(8,128)(2,1)S(1)}, u32[]{:S(2)}, u32[]{:S(2)}) async-start(bf16[16,144,36]{1,2,0:T(8,128)(2,1)} %bitcast.2), calls=%async_computation.1 | async-start | bytes 655360 | tf_op jit(solution)/shard_map/all_to_all | solution.py:98
  172.0 4.1 %convolution_convert_fusion.1 = bf16[512,1152]{1,0:T(8,128)(2,1)} fusion(bf16[512,1152]{1,0:T(8,128)(2,1)} %divide_convert_fusion, bf16[1152,1152]{1,0:T(8,128)(2,1)S(1)} %copy-done), kind=kOutput, calls=%fused_computation.7 | convolution fusion | flops 1359544320 | bytes 5013504 | tf_op jit(solution)/shard_map/dot_general | solution.py:18
  176.2 8.4 %all-to-all-done.1 = bf16[16,144,36]{1,2,0:T(8,128)(2,1)S(1)} async-done(((bf16[16,144,36]{1,2,0:T(8,128)(2,1)}), bf16[16,144,36]{1,2,0:T(8,128)(2,1)S(1)}, u32[]{:S(2)}, u32[]{:S(2)}) %all-to-all-start.1) | async-done | bytes 165920 | tf_op jit(solution)/shard_map/all_to_all | solution.py:98
  (31 shorter events, 4.3 us)
Async XLA Ops:
  0.6 10.4 %copy-start = (bf16[1152,1152]{1,0:T(8,128)(2,1)S(1)}, bf16[1152,1152]{1,0:T(8,128)(2,1)}, u32[]{:S(2)}) copy-start(bf16[1152,1152]{1,0:T(8,128)(2,1)} %param.6) | copy-start | bytes 7962628
  0.6 10.4 %copy-start.3 = (bf16[512,1152]{1,0:T(8,128)(2,1)S(1)}, bf16[512,1152]{1,0:T(8,128)(2,1)}, u32[]{:S(2)}) copy-start(bf16[512,1152]{1,0:T(8,128)(2,1)} %param.5) | copy-start | bytes 3538948
  0.7 76.2 %collective-permute-start.3 = (bf16[512,1152]{1,0:T(8,128)(2,1)}, bf16[512,1152]{1,0:T(8,128)(2,1)}, u32[]{:S(2)}, u32[]{:S(2)}) collective-permute-start(bf16[512,1152]{1,0:T(8,128)(2,1)} %param.4), channel_id=1, source_target_pairs={{0,4},{1,5},{2,6},{3,7},{4,0},{5,1},{6,2},{7,3},{8,12},{9,13},{10,... | collective-permute-start | bytes 3538952 | tf_op jit(solution)/shard_map/ppermute | solution.py:14
  4.7 39.3 %collective-permute-start.5 = (bf16[256,1152]{1,0:T(8,128)(2,1)}, bf16[256,1152]{1,0:T(8,128)(2,1)}, u32[]{:S(2)}, u32[]{:S(2)}) collective-permute-start(bf16[256,1152]{1,0:T(8,128)(2,1)} %get-tuple-element.4), channel_id=1, source_target_pairs={{0,128},{8,136},{16,144},{24,152},{32,160},{40,168},{48,176},{56,1... | collective-permute-start | bytes 1769480 | tf_op jit(solution)/shard_map/ppermute | solution.py:14
  11.0 60.4 %collective-permute-start.4 = (bf16[256,1152]{1,0:T(8,128)(2,1)}, bf16[256,1152]{1,0:T(8,128)(2,1)}, u32[]{:S(2)}, u32[]{:S(2)}) collective-permute-start(bf16[256,1152]{1,0:T(8,128)(2,1)} %get-tuple-element.3), channel_id=1, source_target_pairs={{0,128},{8,136},{16,144},{24,152},{32,160},{40,168},{48,176},{56,1... | collective-permute-start | bytes 1769480 | tf_op jit(solution)/shard_map/ppermute | solution.py:14
  13.0 1.8 copy-start.2
  14.7 9.0 %copy-start.1 = (bf16[512,1152]{1,0:T(8,128)(2,1)S(1)}, bf16[512,1152]{1,0:T(8,128)(2,1)}, u32[]{:S(2)}) copy-start(bf16[512,1152]{1,0:T(8,128)(2,1)} %param.4) | copy-start | bytes 3538948
  14.7 9.3 %copy-start.4 = (s32[1,512]{1,0:T(1,128)S(1)}, s32[1,512]{1,0:T(1,128)}, u32[]{:S(2)}) copy-start(s32[1,512]{1,0:T(1,128)} %param.7) | copy-start | bytes 6148
  14.7 89.3 %collective-permute-start = (bf16[512,1152]{1,0:T(8,128)(2,1)}, bf16[512,1152]{1,0:T(8,128)(2,1)}, u32[]{:S(2)}, u32[]{:S(2)}) collective-permute-start(bf16[512,1152]{1,0:T(8,128)(2,1)} %fusion.145), channel_id=1, source_target_pairs={{0,4},{1,5},{2,6},{3,7},{4,0},{5,1},{6,2},{7,3},{8,12},{9,13},{10,... | collective-permute-start | bytes 3538952 | tf_op jit(solution)/shard_map/ppermute | solution.py:14
  17.8 81.7 %collective-permute-start.2 = (bf16[256,1152]{1,0:T(8,128)(2,1)}, bf16[256,1152]{1,0:T(8,128)(2,1)}, u32[]{:S(2)}, u32[]{:S(2)}) collective-permute-start(bf16[256,1152]{1,0:T(8,128)(2,1)} %get-tuple-element.6), channel_id=1, source_target_pairs={{0,128},{8,136},{16,144},{24,152},{32,160},{40,168},{48,176},{56,1... | collective-permute-start | bytes 1769480 | tf_op jit(solution)/shard_map/ppermute | solution.py:14
  44.0 78.1 %collective-permute-start.1 = (bf16[256,1152]{1,0:T(8,128)(2,1)}, bf16[256,1152]{1,0:T(8,128)(2,1)}, u32[]{:S(2)}, u32[]{:S(2)}) collective-permute-start(bf16[256,1152]{1,0:T(8,128)(2,1)} %get-tuple-element.5), channel_id=1, source_target_pairs={{0,128},{8,136},{16,144},{24,152},{32,160},{40,168},{48,176},{56,1... | collective-permute-start | bytes 1769480 | tf_op jit(solution)/shard_map/ppermute | solution.py:14
  99.5 10.5 %collective-permute-start.6 = (bf16[1152,576]{0,1:T(8,128)(2,1)}, bf16[1152,576]{0,1:T(8,128)(2,1)}, u32[]{:S(2)}, u32[]{:S(2)}) collective-permute-start(bf16[1152,576]{0,1:T(8,128)(2,1)} %convolution_convert_fusion), channel_id=1, source_target_pairs={{0,8},{8,0},{16,24},{24,16},{32,40},{40,32},{48,56},{56,48},{64,72... | collective-permute-start | bytes 3981320 | tf_op jit(solution)/shard_map/ppermute | solution.py:14
  117.6 25.5 %all-to-all-start = ((bf16[8,144,576]{2,1,0:T(8,128)(2,1)}), bf16[8,144,576]{2,1,0:T(8,128)(2,1)}, u32[]{:S(2)}, u32[]{:S(2)}) async-start(bf16[8,144,576]{2,1,0:T(8,128)(2,1)} %bitcast.28), calls=%async_computation | async-start | bytes 2949120 | tf_op jit(solution)/shard_map/all_to_all | solution.py:94
  145.7 38.9 %all-to-all-start.1 = ((bf16[16,144,36]{1,2,0:T(8,128)(2,1)}), bf16[16,144,36]{1,2,0:T(8,128)(2,1)S(1)}, u32[]{:S(2)}, u32[]{:S(2)}) async-start(bf16[16,144,36]{1,2,0:T(8,128)(2,1)} %bitcast.2), calls=%async_computation.1 | async-start | bytes 655360 | tf_op jit(solution)/shard_map/all_to_all | solution.py:98

commit v2 on v1

v2 whole, which is shorter than its diff:
```python
import functools

import jax
import jax.numpy as jnp
from jax import lax
from jax.experimental import pallas as pl
from jax.experimental.pallas import tpu as pltpu
from jax.sharding import PartitionSpec as P

scale_logit = 8.0
bias_logit = -2.0
f32 = jnp.float32
bf16 = jnp.bfloat16
MIB = 1 << 20
X_ONE = 6e9
X_END = 3e9


def from_partner(block, axis, mask):
    count = lax.axis_size(axis)
    return lax.ppermute(block, axis, [(low, low ^ mask) for low in range(count)])


def nt(a, b):
    return lax.dot_general(a, b, (((1,), (1,)), ((), ())), preferred_element_type=f32)


def tn(a, b):
    return lax.dot_general(a, b, (((0,), (0,)), ((), ())), preferred_element_type=f32)


def nn(a, b):
    return jnp.dot(a, b, preferred_element_type=f32)


def unit(block):
    wide = block.astype(f32)
    norm = jnp.sqrt(jnp.sum(wide * wide, axis=-1, keepdims=True) + 1e-06)
    return wide / norm, norm


def unpaired(products):
    return (scale_logit / (1.0 + jnp.exp(-bias_logit - scale_logit * products))).astype(bf16)


def paired(products, labels):
    logits = scale_logit * products + bias_logit
    size = scale_logit / (1.0 + jnp.exp(jnp.where(labels, logits, -logits)))
    return jnp.where(labels, -size, size).astype(bf16)


def tiles(rows, size):
    return [slice(at, at + size) for at in range(0, rows, size)]


def text_kernel(txt_ref, head_ref, mine_ref, theirs_ref, that_ref, tnorm_ref, zt_ref, low_ref, high_ref, my_ref, their_ref, choose):
    width = head_ref.shape[0]

    @pl.when(pl.program_id(0) == 0)
    def _():
        for k, source_ref in enumerate((mine_ref, theirs_ref)):
            index = lax.broadcasted_iota(jnp.int32, (width, source_ref.shape[1]), 0)
            choose[k] = jnp.where(source_ref[...] == index, 1.0, 0.0).astype(bf16)

    txt = txt_ref[...]
    u = nn(txt, head_ref[...])
    tnorm = jnp.sqrt(jnp.sum(u * u, axis=-1, keepdims=True) + 1e-06)
    that = u / tnorm
    that_ref[...] = that
    tnorm_ref[...] = tnorm
    zt_ref[...] = that.astype(bf16)

    @pl.when(pl.program_id(0) == 0)
    def _():
        low_ref[...] = that.astype(bf16)

    @pl.when(pl.program_id(0) == 1)
    def _():
        high_ref[...] = that.astype(bf16)

    my_ref[...] = nn(txt, choose[0]).astype(bf16)
    their_ref[...] = nn(txt, choose[1]).astype(bf16)


def load_units(pieces, zi):
    at = 0
    for piece in pieces:
        zi[at : at + piece.shape[0], :] = unit(piece[...])[0].astype(bf16)
        at += piece.shape[0]


def text_main_kernel(tile, img_ref, two_ref, one_ref, zt_ref, across_ref, zi_ref, dzt_ref, zi):
    load_units([img_ref], zi_ref)
    load_units([two_ref, one_ref], zi)
    for t in tiles(zt_ref.shape[0], tile):
        zt = zt_ref[t, :]
        products = nt(zt, zi_ref[...])
        index = lax.broadcasted_iota(jnp.int32, products.shape, 0) + t.start
        total = nn(paired(products, across_ref[...] == index), zi_ref[...])
        dzt_ref[t, :] = total + nn(unpaired(nt(zt, zi[...])), zi[...])


def text_end_kernel(tile, count, *refs):
    pieces = refs[:count]
    zt_ref, dzt_ref, that_ref, tnorm_ref, txt_ref, du_ref, head_ref, zi = refs[count:]
    load_units(pieces, zi)
    for t in tiles(zt_ref.shape[0], tile):
        dsc = unpaired(nt(zt_ref[t, :], zi[...]))
        dzt = dzt_ref[t, :] + nn(dsc, zi[...])
        that = that_ref[t, :]
        along = jnp.sum(that * dzt, axis=-1, keepdims=True)
        du_ref[t, :] = ((dzt - that * along) / tnorm_ref[t, :]).astype(bf16)
    for t in tiles(du_ref.shape[1], 384):
        head_ref[t, :] = tn(du_ref[:, t], txt_ref[...]).astype(bf16)


def head_kernel(du_ref, txt_ref, got_ref, out_ref):
    for t in tiles(du_ref.shape[1], 384):
        mine = tn(du_ref[:, t], txt_ref[...])
        out_ref[t, :] = (mine + got_ref[t, :].astype(f32)).astype(bf16)


def txt_grad_kernel(tile, du_ref, head_ref, out_ref):
    for t in tiles(du_ref.shape[0], tile):
        out_ref[t, :] = nt(du_ref[t, :], head_ref[...]).astype(bf16)


def gather_kernel(pad, fold, got_ref, out_ref):
    total = got_ref[0].astype(f32)
    for k in range(1, got_ref.shape[0]):
        total = total + got_ref[k].astype(f32)
    high = total.shape[0] // fold
    for i in range(out_ref.shape[0]):
        cut = [total[high * k : high * (k + 1), pad * i : pad * (i + 1)] for k in range(fold)]
        rest = out_ref.shape[2] - fold * pad
        cut.append(jnp.zeros((high, rest), f32))
        out_ref[i] = jnp.concatenate(cut, axis=1).astype(bf16)


def finish_kernel(pad, fold, devices, got_ref, out_ref):
    total = got_ref[0].astype(f32)
    for k in range(1, got_ref.shape[0]):
        total = total + got_ref[k].astype(f32)
    turned = (total * (1.0 / devices)).T
    rows = out_ref.shape[0]
    cut = [turned[pad * k : pad * k + rows] for k in range(fold)]
    out_ref[...] = jnp.concatenate(cut, axis=1)


def image_main_kernel(tile, zi_ref, zt_ref, low_ref, high_ref, down_ref, dzi_ref, two_ref):
    two_ref[: low_ref.shape[0], :] = low_ref[...]
    two_ref[low_ref.shape[0] :, :] = high_ref[...]
    for t in tiles(zi_ref.shape[0], tile):
        zi = zi_ref[t, :]
        products = nt(zi, zt_ref[...])
        index = lax.broadcasted_iota(jnp.int32, products.shape, 1)
        total = nn(paired(products, down_ref[t, :] == index), zt_ref[...])
        dzi_ref[t, :] = total + nn(unpaired(nt(zi, two_ref[...])), two_ref[...])


def image_side_kernel(tile, one_ref, zi_ref, dzi_ref, out_ref):
    for t in tiles(zi_ref.shape[0], tile):
        dsc = unpaired(nt(zi_ref[t, :], one_ref[...]))
        out_ref[t, :] = dzi_ref[t, :] + nn(dsc, one_ref[...])


def image_end_kernel(tile, one_ref, zi_ref, dzi_ref, img_ref, out_ref):
    for t in tiles(zi_ref.shape[0], tile):
        dsc = unpaired(nt(zi_ref[t, :], one_ref[...]))
        dzi = dzi_ref[t, :] + nn(dsc, one_ref[...])
        ihat, inorm = unit(img_ref[t, :])
        along = jnp.sum(ihat * dzi, axis=-1, keepdims=True)
        out_ref[t, :] = ((dzi - ihat * along) / inorm).astype(bf16)


def call(kernel, outs, args, scratch=(), aliases=None, name=None, flops=1):
    return pl.pallas_call(
        kernel,
        out_shape=outs,
        scratch_shapes=list(scratch),
        input_output_aliases=aliases or {},
        compiler_params=pltpu.CompilerParams(vmem_limit_bytes=12 * MIB),
        cost_estimate=pl.CostEstimate(flops=flops, bytes_accessed=1, transcendentals=0),
        name=name,
    )(*args)


def shards(img_emb, txt_feat, head_weight, positive):
    rows, width = img_emb.shape
    n_row = lax.axis_size("row")
    n_col = lax.axis_size("col")
    share_rows = width // n_row
    share_cols = width // n_col
    depth = n_row // 4
    tile = min(128, rows)
    shape = jax.ShapeDtypeStruct

    def after(value, *others):
        return lax.optimization_barrier((value,) + others)[0]

    half = rows // 2
    img_a, img_b = img_emb[:half], img_emb[half:]
    txt_feat = after(txt_feat, img_a, img_b)
    img_two = from_partner(after(img_emb, img_a, img_b), "col", n_col // 2)
    img_a = from_partner(img_a, "row", n_row // 2)
    img_b = from_partner(img_b, "row", n_row // 2)

    core = lax.axis_index("row") & 1
    pad = -(-share_rows // 8) * 8
    lanes = 2 * depth * pad
    lane = jnp.arange(lanes, dtype=jnp.int32)
    place = lane // pad
    inner = lane % pad
    block = (place % depth) * 4 + (place // depth) * 2

    def sources(which):
        return jnp.where(inner < share_rows, (block + which) * share_rows + inner, -1)[None, :]

    step = rows // 2
    that, tnorm, zt, zt_low, zt_high, txt_mine, txt_theirs = pl.pallas_call(
        text_kernel,
        grid=(2,),
        in_specs=[
            pl.BlockSpec((step, width), lambda i: (i, 0)),
            pl.BlockSpec((width, width), lambda i: (0, 0)),
            pl.BlockSpec((1, lanes), lambda i: (0, 0)),
            pl.BlockSpec((1, lanes), lambda i: (0, 0)),
        ],
        out_specs=[
            pl.BlockSpec((step, width), lambda i: (i, 0)),
            pl.BlockSpec((step, 1), lambda i: (i, 0)),
            pl.BlockSpec((step, width), lambda i: (i, 0)),
            pl.BlockSpec((step, width), lambda i: (0, 0)),
            pl.BlockSpec((step, width), lambda i: (0, 0)),
            pl.BlockSpec((step, lanes), lambda i: (i, 0)),
            pl.BlockSpec((step, lanes), lambda i: (i, 0)),
        ],
        out_shape=[
            shape((rows, width), f32),
            shape((rows, 1), f32),
            shape((rows, width), bf16),
            shape((step, width), bf16),
            shape((step, width), bf16),
            shape((rows, lanes), bf16),
            shape((rows, lanes), bf16),
        ],
        scratch_shapes=[pltpu.VMEM((2, width, lanes), bf16)],
        compiler_params=pltpu.CompilerParams(vmem_limit_bytes=16 * MIB),
        cost_estimate=pl.CostEstimate(flops=1, bytes_accessed=1, transcendentals=0),
        name="text",
    )(txt_feat, head_weight, sources(core), sources(1 - core))
    txt_two = [from_partner(part, "col", n_col // 2) for part in (zt_low, zt_high)]

    wide = shape((rows, width), f32)
    narrow = shape((rows, width), bf16)
    zi, dzt = call(
        functools.partial(text_main_kernel, tile),
        [narrow, wide],
        [img_emb, img_two, img_a, zt, positive],
        [pltpu.VMEM((rows + half, width), bf16)],
        name="text_main",
    )
    du, head = call(
        functools.partial(text_end_kernel, tile, 1),
        [narrow, shape((width, lanes), bf16)],
        [img_b, zt, dzt, that, tnorm, txt_theirs],
        [pltpu.VMEM((half, width), bf16)],
        name="text_end",
    )
    head = from_partner(after(head, *txt_two), "row", 1)
    head = call(
        head_kernel,
        shape((width, lanes), bf16),
        [du, txt_mine, head],
        name="head",
    )
    txt_a = from_partner(after(zt_low, du), "row", n_row // 2)
    du_late = after(du, head)
    head = lax.all_to_all(head.reshape(n_col, share_cols, lanes), "col", 0, 0, tiled=True)
    txt_grad = call(
        functools.partial(txt_grad_kernel, tile), narrow, [du_late, head_weight], name="txt_grad"
    )
    dzi = call(
        functools.partial(image_main_kernel, tile),
        wide,
        [zi, zt, *txt_two, after(positive, txt_grad).reshape(rows, 1)],
        [pltpu.VMEM((rows, width), bf16)],
        name="image_main",
    )
    dzi = call(
        functools.partial(image_side_kernel, tile),
        wide,
        [txt_a, zi, dzi],
        (),
        {2: 0},
        name="image_one",
        flops=int(X_ONE),
    )
    head = after(head, dzi)
    txt_b = from_partner(after(zt_high, dzi), "row", n_row // 2)
    fold = 3
    head = call(
        functools.partial(gather_kernel, pad, fold),
        shape((2 * depth, share_cols // fold, 128), bf16),
        [head],
        name="gather",
    )
    groups = [[z * 4 + y * 2 + c for y in range(2) for z in range(depth)] for c in range(2)]
    head = lax.all_to_all(head, "row", 0, 0, axis_index_groups=groups, tiled=True)
    img_grad = call(
        functools.partial(image_end_kernel, tile),
        narrow,
        [txt_b, zi, dzi, img_emb],
        name="image_end",
        flops=int(X_END),
    )
    head_grad = call(
        functools.partial(finish_kernel, pad, fold, n_row * n_col),
        shape((share_rows, share_cols), f32),
        [after(head, img_grad)],
        name="finish",
    )
    return (img_grad, txt_grad, head_grad)


def solution(mesh):
    return jax.shard_map(
        shards,
        mesh=mesh,
        in_specs=(P(("row", "col"), None), P(("row", "col"), None), P(), P(("row", "col"), None)),
        out_specs=(P(("row", "col"), None), P(("row", "col"), None), P("row", "col")),
        check_vma=False,
    )
```

time: 186 us -> 141 us (0.76)
  matrix products: 59.1 us -> 0 us
  Pallas kernels: 0 us -> 41.5 us
  other arithmetic: 15.6 us -> 0.04 us
  starting transfers between devices: 51.3 us -> 36.7 us
  local copies, waits for them, and re-layouts: 8.56 us -> 13.3 us
  waiting for transfers between devices: 50 us -> 46.7 us
    dot_general x13 -> x0, matrix products: 59.1 us -> none  [the longest x6 30.1 us: columns_by_columns(): lax.dot_general(a, b, (((0,), (0,)), ((), ())), preferred_element_type=f32)]
    pallas_call x0 -> x10, Pallas kernels: none -> 41.5 us  [the longest x9 35.6 us: call(): pl.pallas_call(kernel, out_shape=outs, scratch_shapes=list(scratch), inpu...]
    all_to_all x1, starting transfers between devices: 26.3 us -> 11.4 us  [shards(): lax.all_to_all(head, 'row', 0, 0, axis_index_groups=groups, tiled=True)]
    all_to_all x1, waiting for transfers between devices: 11.1 us -> 0.01 us  [shards(): lax.all_to_all(head.reshape(n_col, share_cols, lanes), 'col', 0, 0, tiled...]
    ppermute x7 -> x8, waiting for transfers between devices: 30.5 us -> 41 us  [from_partner(): lax.ppermute(block, axis, [(low, low ^ mask) for low in range(count)])]
    unnamed x10 -> x34, local copies, waits for them, and re-layouts: 0.24 us -> 10.7 us
    convert_element_type x3 -> x0, other arithmetic: 8.86 us -> none  [the longest x1 3.85 us: shards(): ((dzt - that * jnp.sum(that * dzt, axis=-1, keepdims=True)) / tnorm).asty...]
    reduce_sum x6 -> x0, other arithmetic: 6.08 us -> none  [the longest x4 4.4 us: unit(): norm = jnp.sqrt(jnp.sum(wide * wide, axis=-1, keepdims=True) + 1e-06)]
  transfers between devices with their start and end apart: 9 -> 10, of which waited for: 4 -> 4; matrix products, arithmetic and copies ran while one was open for 43% -> 0% of each run, Pallas kernels for 0% -> 29%
where the time goes in v2:
time: 141 us; the launch traced here: 139 us
  waiting for transfers between devices  46.7 us (33%)
  Pallas kernels  41.5 us (29%)
  starting transfers between devices  36.7 us (26%)
  local copies, waits for them, and re-layouts  13.3 us (9%)
    ppermute x8, waiting for transfers between devices, from_partner(): lax.ppermute(block, axis, [(low, low ^ mask) for low in range(count)])  41 us
    pallas_call x9, Pallas kernels, call(): pl.pallas_call(kernel, out_shape=outs, scratch_shapes=list(scratch), inpu...  35.6 us
    ppermute x8, starting transfers between devices, from_partner(): lax.ppermute(block, axis, [(low, low ^ mask) for low in range(count)])  20.6 us
    all_to_all x1, starting transfers between devices, shards(): lax.all_to_all(head, 'row', 0, 0, axis_index_groups=groups, tiled=True)  11.4 us
    unnamed x34, local copies, waits for them, and re-layouts  10.7 us
    pallas_call x1, Pallas kernels, shards(): pl.pallas_call(text_kernel, grid=(2,), in_specs=[pl.BlockSpec((step, widt...  5.98 us
    all_to_all x1, waiting for transfers between devices, shards(): lax.all_to_all(head, 'row', 0, 0, axis_index_groups=groups, tiled=True)  5.69 us
    all_to_all x1, starting transfers between devices, shards(): lax.all_to_all(head.reshape(n_col, share_cols, lanes), 'col', 0, 0, tiled...  4.77 us
  transfers between devices with their start and end apart: 10, of which 4 were waited for; matrix products, arithmetic and copies ran while one was open for 0% of the time, Pallas kernels for 29%

profile of v2, /device:TPU:32, one launch (start us, length us, event | category | flops | bytes accessed | tf_op | source)
XLA Modules:
  0.0 139.2 jit_solution(8955258080210779136)
XLA Ops:
  0.7 2.5 %fusion.2 = (bf16[256,1152]{1,0:T(8,128)(2,1)}, bf16[256,1152]{1,0:T(8,128)(2,1)}) fusion(bf16[512,1152]{1,0:T(8,128)(2,1)} %img_ref.3), kind=kLoop, calls=%fused_computation.14 | loop fusion | bytes 2359296 | tf_op jit(solution)/shard_map/slice | solution.py:202
  3.1 1.6 %collective-permute-start.1 = (bf16[512,1152]{1,0:T(8,128)(2,1)S(1)}, bf16[512,1152]{1,0:T(8,128)(2,1)S(1)}, u32[]{:S(2)}, u32[]{:S(2)}) collective-permute-start(bf16[512,1152]{1,0:T(8,128)(2,1)S(1)} %copy-done.5), channel_id=1, source_target_pairs={{0,4},{1,5},{2,6},{3,7},{4,0},{5,1},{6,2},{7,3},{8,12},{9,13},{10,... | collective-permute-start | bytes 3538952 | tf_op jit(solution)/shard_map/ppermute | solution.py:21
  4.7 6.3 %collective-permute-start.2 = (bf16[256,1152]{1,0:T(8,128)(2,1)}, bf16[256,1152]{1,0:T(8,128)(2,1)}, u32[]{:S(2)}, u32[]{:S(2)}) collective-permute-start(bf16[256,1152]{1,0:T(8,128)(2,1)} %get-tuple-element.44), channel_id=1, source_target_pairs={{0,128},{8,136},{16,144},{24,152},{32,160},{40,168},{48,176},{56,1... | collective-permute-start | bytes 1769480 | tf_op jit(solution)/shard_map/ppermute | solution.py:21
  11.1 1.7 %copy-done = bf16[1152,1152]{1,0:T(8,128)(2,1)S(1)} copy-done((bf16[1152,1152]{1,0:T(8,128)(2,1)S(1)}, bf16[1152,1152]{1,0:T(8,128)(2,1)}, u32[]{:S(2)}) %copy-start) | copy-done | bytes 2654232
  12.9 6.0 %text.1 = (f32[512,1152]{1,0:T(8,128)S(1)}, f32[512,1]{1,0:T(8,128)S(1)}, bf16[512,1152]{1,0:T(8,128)(2,1)S(1)}, bf16[256,1152]{1,0:T(8,128)(2,1)}, bf16[256,115...) custom-call(bf16[512,1152]{1,0:T(8,128)(2,1)S(1)} %copy-done.9, ...), custom_call_target="tpu_custom_call" | custom-call | flops 1 | bytes 1 | tf_op jit(solution)/shard_map/text/pallas_call | solution.py:220
  18.8 0.4 collective-permute-start.4
  19.3 1.6 %collective-permute-start.5 = (bf16[256,1152]{1,0:T(8,128)(2,1)}, bf16[256,1152]{1,0:T(8,128)(2,1)S(1)}, u32[]{:S(2)}, u32[]{:S(2)}) collective-permute-start(bf16[256,1152]{1,0:T(8,128)(2,1)} %get-tuple-element.40), channel_id=1, source_target_pairs={{0,4},{1,5},{2,6},{3,7},{4,0},{5,1},{6,2},{7,3},{8,12},{9,13},{10,... | collective-permute-start | bytes 1769480 | tf_op jit(solution)/shard_map/ppermute | solution.py:21
  20.9 23.2 %collective-permute-done.2.one_ref = bf16[256,1152]{1,0:T(8,128)(2,1)} collective-permute-done((bf16[256,1152]{1,0:T(8,128)(2,1)}, bf16[256,1152]{1,0:T(8,128)(2,1)}, u32[]{:S(2)}, u32[]{:S(2)}) %collective-permute-start.2) | collective-permute-done | bytes 589856 | tf_op jit(solution)/shard_map/ppermute | solution.py:21
  44.1 7.9 %text_main.1 = (bf16[512,1152]{1,0:T(8,128)(2,1)S(1)}, f32[512,1152]{1,0:T(8,128)S(1)}) custom-call(bf16[512,1152]{1,0:T(8,128)(2,1)S(1)} %copy-done.5, bf16[512,1152]{1,0:T(8,128)(2,1)S(1)} %collective-permute-done.1.two_ref, bf16[256,1152]{1,0:T(8,128)(2,1)} %collective-permute-done.2.one_ref, bf16[512,1152]{1,0:T(8,128)(2,1)S(1)} %get-tuple-element.26.zt_ref.refs_1_, ...), custom_call_target="tpu_custom_call" | custom-call | flops 1 | bytes 1 | tf_op jit(solution)/shard_map/text_main/pallas_call | solution.py:177
  52.0 1.0 copy-done.10
  53.0 9.6 %collective-permute-done.refs_0_ = bf16[256,1152]{1,0:T(8,128)(2,1)} collective-permute-done((bf16[256,1152]{1,0:T(8,128)(2,1)}, bf16[256,1152]{1,0:T(8,128)(2,1)}, u32[]{:S(2)}, u32[]{:S(2)}) %collective-permute-start) | collective-permute-done | bytes 589856 | tf_op jit(solution)/shard_map/ppermute | solution.py:21
  62.6 5.0 %text_end.1 = (bf16[512,1152]{1,0:T(8,128)(2,1)S(1)}, bf16[1152,640]{1,0:T(8,128)(2,1)S(1)}) custom-call(bf16[256,1152]{1,0:T(8,128)(2,1)} %collective-permute-done.refs_0_, bf16[512,1152]{1,0:T(8,128)(2,1)S(1)} %get-tuple-element.26.zt_ref.refs_1_, f32[512,1152]{1,0:T(8,128)S(1)} %get-tuple-element.28.refs_2_, f32[512,1152]{1,0:T(8,128)S(1)} %get-tuple-element.29.refs_3_, ...), custom_call_target="tpu_custom_call" | custom-call | flops 1 | bytes 1 | tf_op jit(solution)/shard_map/text_end/pallas_call | solution.py:177
  67.7 5.5 %collective-permute-start.3 = (bf16[256,1152]{1,0:T(8,128)(2,1)}, bf16[256,1152]{1,0:T(8,128)(2,1)}, u32[]{:S(2)}, u32[]{:S(2)}) collective-permute-start(bf16[256,1152]{1,0:T(8,128)(2,1)} %get-tuple-element.33), channel_id=1, source_target_pairs={{0,128},{8,136},{16,144},{24,152},{32,160},{40,168},{48,176},{56,1... | collective-permute-start | bytes 1769480 | tf_op jit(solution)/shard_map/ppermute | solution.py:21
  73.3 1.1 head.1
  74.4 1.1 copy-done.4
  75.5 4.8 %all-to-all-start = ((bf16[8,144,640]{2,1,0:T(8,128)(2,1)}), bf16[8,144,640]{2,1,0:T(8,128)(2,1)}, u32[]{:S(2)}, u32[]{:S(2)}) async-start(bf16[8,144,640]{2,1,0:T(8,128)(2,1)} %bitcast.2), calls=%async_computation | async-start | bytes 2949120 | tf_op jit(solution)/shard_map/all_to_all | solution.py:279
  80.3 1.3 copy-done.8
  81.6 4.3 %txt_grad.1 = bf16[512,1152]{1,0:T(8,128)(2,1)} custom-call(bf16[512,1152]{1,0:T(8,128)(2,1)S(1)} %copy-done.8, bf16[1152,1152]{1,0:T(8,128)(2,1)S(1)} %copy-done.1), custom_call_target="tpu_custom_call" | custom-call | flops 1 | bytes 1 | tf_op jit(solution)/shard_map/txt_grad/pallas_call | solution.py:177
  86.0 1.3 copy-done.3
  87.3 1.3 copy-done.11
  88.5 1.1 copy-done.15
  89.6 5.4 %image_main.1.dzi_ref = f32[512,1152]{1,0:T(8,128)S(1)} custom-call(bf16[512,1152]{1,0:T(8,128)(2,1)S(1)} %copy-done.11, bf16[512,1152]{1,0:T(8,128)(2,1)S(1)} %copy-done.3, bf16[256,1152]{1,0:T(8,128)(2,1)S(1)} %collective-permute-done.4.low_ref, bf16[256,1152]{1,0:T(8,128)(2,1)S(1)} %copy-done.15, s32[512,1]{1,0:T(8,128)S(1)} %copy.8.down_ref), custom_call_target="tpu_custom_call" | custom-call | flops 1 | bytes 1 | tf_op jit(solution)/shard_map/image_main/pallas_call | solution.py:177
  95.0 3.6 %image_one.1.dzi_ref = f32[512,1152]{1,0:T(8,128)S(1)} custom-call(bf16[256,1152]{1,0:T(8,128)(2,1)} %collective-permute-done.3.one_ref, bf16[512,1152]{1,0:T(8,128)(2,1)S(1)} %copy-done.11, f32[512,1152]{1,0:T(8,128)S(1)} %image_main.1.dzi_ref), custom_call_target="tpu_custom_call", output_to_operand_aliasing={{}: (2, {})} | custom-call | flops 6000000000 | bytes 1 | tf_op jit(solution)/shard_map/image_one/pallas_call | solution.py:177
  98.6 5.1 %collective-permute-start.7 = (bf16[256,1152]{1,0:T(8,128)(2,1)}, bf16[256,1152]{1,0:T(8,128)(2,1)}, u32[]{:S(2)}, u32[]{:S(2)}) collective-permute-start(bf16[256,1152]{1,0:T(8,128)(2,1)} %get-tuple-element.40), channel_id=1, source_target_pairs={{0,128},{8,136},{16,144},{24,152},{32,160},{40,168},{48,176},{56,1... | collective-permute-start | bytes 1769480 | tf_op jit(solution)/shard_map/ppermute | solution.py:21
  103.6 1.7 %gather.1 = bf16[16,48,128]{2,1,0:T(8,128)(2,1)S(1)} custom-call(bf16[8,144,640]{2,1,0:T(8,128)(2,1)} %all-to-all-done.got_ref), custom_call_target="tpu_custom_call" | custom-call | flops 1 | bytes 1 | tf_op jit(solution)/shard_map/gather/pallas_call | solution.py:177
  105.4 0.7 copy-done.13
  106.0 11.4 %all-to-all-start.1 = ((bf16[16,48,128]{2,1,0:T(8,128)(2,1)}), bf16[16,48,128]{2,1,0:T(8,128)(2,1)}, u32[]{:S(2)}, u32[]{:S(2)}) async-start(bf16[16,48,128]{2,1,0:T(8,128)(2,1)} %copy-done.13), calls=%async_computation.1 | async-start | bytes 393216 | tf_op jit(solution)/shard_map/all_to_all | solution.py:309
  117.4 8.2 %collective-permute-done.7.one_ref = bf16[256,1152]{1,0:T(8,128)(2,1)} collective-permute-done((bf16[256,1152]{1,0:T(8,128)(2,1)}, bf16[256,1152]{1,0:T(8,128)(2,1)}, u32[]{:S(2)}, u32[]{:S(2)}) %collective-permute-start.7) | collective-permute-done | bytes 589856 | tf_op jit(solution)/shard_map/ppermute | solution.py:21
  125.6 1.3 copy-done.12
  126.9 4.9 %image_end.1 = bf16[512,1152]{1,0:T(8,128)(2,1)} custom-call(bf16[256,1152]{1,0:T(8,128)(2,1)} %collective-permute-done.7.one_ref, bf16[512,1152]{1,0:T(8,128)(2,1)S(1)} %copy-done.12, f32[512,1152]{1,0:T(8,128)S(1)} %image_one.1.dzi_ref, bf16[512,1152]{1,0:T(8,128)(2,1)S(1)} %copy-done.6), custom_call_target="tpu_custom_call" | custom-call | flops 3000000000 | bytes 1 | tf_op jit(solution)/shard_map/image_end/pallas_call | solution.py:177
  131.7 5.7 %all-to-all-done.1.got_ref = bf16[16,48,128]{2,1,0:T(8,128)(2,1)} async-done(((bf16[16,48,128]{2,1,0:T(8,128)(2,1)}), bf16[16,48,128]{2,1,0:T(8,128)(2,1)}, u32[]{:S(2)}, u32[]{:S(2)}) %all-to-all-start.1) | async-done | bytes 196640 | tf_op jit(solution)/shard_map/all_to_all | solution.py:309
  137.4 1.7 %finish.1 = f32[36,144]{1,0:T(8,128)} custom-call(bf16[16,48,128]{2,1,0:T(8,128)(2,1)} %all-to-all-done.1.got_ref), custom_call_target="tpu_custom_call" | custom-call | flops 1 | bytes 1 | tf_op jit(solution)/shard_map/finish/pallas_call | solution.py:177
  (35 shorter events, 0.4 us)
Async XLA Ops:
  0.6 2.5 %copy-start.5 = (bf16[512,1152]{1,0:T(8,128)(2,1)S(1)}, bf16[512,1152]{1,0:T(8,128)(2,1)}, u32[]{:S(2)}) copy-start(bf16[512,1152]{1,0:T(8,128)(2,1)} %img_ref.3) | copy-start | bytes 3538948
  0.6 10.5 %copy-start.9 = (bf16[512,1152]{1,0:T(8,128)(2,1)S(1)}, bf16[512,1152]{1,0:T(8,128)(2,1)}, u32[]{:S(2)}) copy-start(bf16[512,1152]{1,0:T(8,128)(2,1)} %txt_ref) | copy-start | bytes 3538948
  3.1 40.9 %collective-permute-start.1 = (bf16[512,1152]{1,0:T(8,128)(2,1)S(1)}, bf16[512,1152]{1,0:T(8,128)(2,1)S(1)}, u32[]{:S(2)}, u32[]{:S(2)}) collective-permute-start(bf16[512,1152]{1,0:T(8,128)(2,1)S(1)} %copy-done.5), channel_id=1, source_target_pairs={{0,4},{1,5},{2,6},{3,7},{4,0},{5,1},{6,2},{7,3},{8,12},{9,13},{10,... | collective-permute-start | bytes 3538952 | tf_op jit(solution)/shard_map/ppermute | solution.py:21
  4.7 39.3 %collective-permute-start.2 = (bf16[256,1152]{1,0:T(8,128)(2,1)}, bf16[256,1152]{1,0:T(8,128)(2,1)}, u32[]{:S(2)}, u32[]{:S(2)}) collective-permute-start(bf16[256,1152]{1,0:T(8,128)(2,1)} %get-tuple-element.44), channel_id=1, source_target_pairs={{0,128},{8,136},{16,144},{24,152},{32,160},{40,168},{48,176},{56,1... | collective-permute-start | bytes 1769480 | tf_op jit(solution)/shard_map/ppermute | solution.py:21
  11.0 51.6 %collective-permute-start = (bf16[256,1152]{1,0:T(8,128)(2,1)}, bf16[256,1152]{1,0:T(8,128)(2,1)}, u32[]{:S(2)}, u32[]{:S(2)}) collective-permute-start(bf16[256,1152]{1,0:T(8,128)(2,1)} %get-tuple-element.43), channel_id=1, source_target_pairs={{0,128},{8,136},{16,144},{24,152},{32,160},{40,168},{48,176},{56,1... | collective-permute-start | bytes 1769480 | tf_op jit(solution)/shard_map/ppermute | solution.py:21
  11.1 1.8 %copy-start = (bf16[1152,1152]{1,0:T(8,128)(2,1)S(1)}, bf16[1152,1152]{1,0:T(8,128)(2,1)}, u32[]{:S(2)}) copy-start(bf16[1152,1152]{1,0:T(8,128)(2,1)} %head_ref.3) | copy-start | bytes 7962628
  12.9 31.2 %copy-start.16 = (s32[1,512]{1,0:T(1,128)S(1)}, s32[1,512]{1,0:T(1,128)}, u32[]{:S(2)}) copy-start(s32[1,512]{1,0:T(1,128)} %across_ref.1) | copy-start | bytes 6148
  18.8 43.8 %copy-start.2 = (bf16[512,1152]{1,0:T(8,128)(2,1)}, bf16[512,1152]{1,0:T(8,128)(2,1)S(1)}, u32[]{:S(2)}) copy-start(bf16[512,1152]{1,0:T(8,128)(2,1)S(1)} %get-tuple-element.26.zt_ref.refs_1_) | copy-start | bytes 3538948
  18.8 48.8 %collective-permute-start.4 = (bf16[256,1152]{1,0:T(8,128)(2,1)}, bf16[256,1152]{1,0:T(8,128)(2,1)S(1)}, u32[]{:S(2)}, u32[]{:S(2)}) collective-permute-start(bf16[256,1152]{1,0:T(8,128)(2,1)} %get-tuple-element.33), channel_id=1, source_target_pairs={{0,4},{1,5},{2,6},{3,7},{4,0},{5,1},{6,2},{7,3},{8,12},{9,13},{10,... | collective-permute-start | bytes 1769480 | tf_op jit(solution)/shard_map/ppermute | solution.py:21
  19.3 48.3 %collective-permute-start.5 = (bf16[256,1152]{1,0:T(8,128)(2,1)}, bf16[256,1152]{1,0:T(8,128)(2,1)S(1)}, u32[]{:S(2)}, u32[]{:S(2)}) collective-permute-start(bf16[256,1152]{1,0:T(8,128)(2,1)} %get-tuple-element.40), channel_id=1, source_target_pairs={{0,4},{1,5},{2,6},{3,7},{4,0},{5,1},{6,2},{7,3},{8,12},{9,13},{10,... | collective-permute-start | bytes 1769480 | tf_op jit(solution)/shard_map/ppermute | solution.py:21
  52.0 1.0 copy-start.10
  67.6 6.8 %copy-start.7 = (bf16[512,1152]{1,0:T(8,128)(2,1)}, bf16[512,1152]{1,0:T(8,128)(2,1)S(1)}, u32[]{:S(2)}) copy-start(bf16[512,1152]{1,0:T(8,128)(2,1)S(1)} %get-tuple-element.38.du_ref) | copy-start | bytes 3538948
  67.6 6.8 %copy-start.14 = (bf16[256,1152]{1,0:T(8,128)(2,1)}, bf16[256,1152]{1,0:T(8,128)(2,1)S(1)}, u32[]{:S(2)}) copy-start(bf16[256,1152]{1,0:T(8,128)(2,1)S(1)} %collective-permute-done.5.high_ref) | copy-start | bytes 1769476
  67.6 5.6 %collective-permute-start.6 = (bf16[1152,640]{1,0:T(8,128)(2,1)S(1)}, bf16[1152,640]{1,0:T(8,128)(2,1)S(1)}, u32[]{:S(2)}, u32[]{:S(2)}) collective-permute-start(bf16[1152,640]{1,0:T(8,128)(2,1)S(1)} %get-tuple-element.37), channel_id=1, source_target_pairs={{0,8},{8,0},{16,24},{24,16},{32,40},{40,32},{48,56},{56,48},{64,72... | collective-permute-start | bytes 4423688 | tf_op jit(solution)/shard_map/ppermute | solution.py:21
  67.7 27.2 %collective-permute-start.3 = (bf16[256,1152]{1,0:T(8,128)(2,1)}, bf16[256,1152]{1,0:T(8,128)(2,1)}, u32[]{:S(2)}, u32[]{:S(2)}) collective-permute-start(bf16[256,1152]{1,0:T(8,128)(2,1)} %get-tuple-element.33), channel_id=1, source_target_pairs={{0,128},{8,136},{16,144},{24,152},{32,160},{40,168},{48,176},{56,1... | collective-permute-start | bytes 1769480 | tf_op jit(solution)/shard_map/ppermute | solution.py:21
  74.4 1.1 copy-start.4
  75.5 4.8 %copy-start.1 = (bf16[1152,1152]{1,0:T(8,128)(2,1)S(1)}, bf16[1152,1152]{1,0:T(8,128)(2,1)}, u32[]{:S(2)}) copy-start(bf16[1152,1152]{1,0:T(8,128)(2,1)} %head_ref.3) | copy-start | bytes 7962628
  75.5 28.1 %all-to-all-start = ((bf16[8,144,640]{2,1,0:T(8,128)(2,1)}), bf16[8,144,640]{2,1,0:T(8,128)(2,1)}, u32[]{:S(2)}, u32[]{:S(2)}) async-start(bf16[8,144,640]{2,1,0:T(8,128)(2,1)} %bitcast.2), calls=%async_computation | async-start | bytes 2949120 | tf_op jit(solution)/shard_map/all_to_all | solution.py:279
  80.3 1.3 copy-start.8
  86.0 1.3 copy-start.3
  87.3 1.3 copy-start.11
  88.5 1.1 copy-start.15
  98.6 27.0 %copy-start.6 = (bf16[512,1152]{1,0:T(8,128)(2,1)S(1)}, bf16[512,1152]{1,0:T(8,128)(2,1)}, u32[]{:S(2)}) copy-start(bf16[512,1152]{1,0:T(8,128)(2,1)} %img_ref.3) | copy-start | bytes 3538948
  98.6 27.0 %collective-permute-start.7 = (bf16[256,1152]{1,0:T(8,128)(2,1)}, bf16[256,1152]{1,0:T(8,128)(2,1)}, u32[]{:S(2)}, u32[]{:S(2)}) collective-permute-start(bf16[256,1152]{1,0:T(8,128)(2,1)} %get-tuple-element.40), channel_id=1, source_target_pairs={{0,128},{8,136},{16,144},{24,152},{32,160},{40,168},{48,176},{56,1... | collective-permute-start | bytes 1769480 | tf_op jit(solution)/shard_map/ppermute | solution.py:21
  105.4 0.7 copy-start.13
  106.0 31.4 %all-to-all-start.1 = ((bf16[16,48,128]{2,1,0:T(8,128)(2,1)}), bf16[16,48,128]{2,1,0:T(8,128)(2,1)}, u32[]{:S(2)}, u32[]{:S(2)}) async-start(bf16[16,48,128]{2,1,0:T(8,128)(2,1)} %copy-done.13), calls=%async_computation.1 | async-start | bytes 393216 | tf_op jit(solution)/shard_map/all_to_all | solution.py:309
  125.6 1.3 copy-start.12

commit v3 on v2

--- a/solution.py
+++ b/solution.py
@@ -12,7 +12,7 @@
 f32 = jnp.float32
 bf16 = jnp.bfloat16
 MIB = 1 << 20
-X_ONE = 6e9
+X_FIRST = 6e9
 X_END = 3e9
 
 
@@ -21,6 +21,11 @@
     return lax.ppermute(block, axis, [(low, low ^ mask) for low in range(count)])
 
 
+def turn(block, by):
+    count = lax.axis_size("row")
+    return lax.ppermute(block, "row", [(at, (at + 4 * by) % count) for at in range(count)])
+
+
 def nt(a, b):
     return lax.dot_general(a, b, (((1,), (1,)), ((), ())), preferred_element_type=f32)
 
@@ -35,8 +40,8 @@
 
 def unit(block):
     wide = block.astype(f32)
-    norm = jnp.sqrt(jnp.sum(wide * wide, axis=-1, keepdims=True) + 1e-06)
-    return wide / norm, norm
+    back = 1.0 / jnp.sqrt(jnp.sum(wide * wide, axis=-1, keepdims=True) + 1e-06)
+    return wide * back, back
 
 
 def unpaired(products):
@@ -53,7 +58,7 @@
     return [slice(at, at + size) for at in range(0, rows, size)]
 
 
-def text_kernel(txt_ref, head_ref, mine_ref, theirs_ref, that_ref, tnorm_ref, zt_ref, low_ref, high_ref, my_ref, their_ref, choose):
+def text_kernel(txt_ref, head_ref, mine_ref, theirs_ref, that_ref, back_ref, zt_ref, low_ref, high_ref, my_ref, their_ref, choose):
     width = head_ref.shape[0]
 
     @pl.when(pl.program_id(0) == 0)
@@ -64,10 +69,10 @@
 
     txt = txt_ref[...]
     u = nn(txt, head_ref[...])
-    tnorm = jnp.sqrt(jnp.sum(u * u, axis=-1, keepdims=True) + 1e-06)
-    that = u / tnorm
+    back = 1.0 / jnp.sqrt(jnp.sum(u * u, axis=-1, keepdims=True) + 1e-06)
+    that = u * back
     that_ref[...] = that
-    tnorm_ref[...] = tnorm
+    back_ref[...] = back
     zt_ref[...] = that.astype(bf16)
 
     @pl.when(pl.program_id(0) == 0)
@@ -89,9 +94,9 @@
         at += piece.shape[0]
 
 
-def text_main_kernel(tile, img_ref, two_ref, one_ref, zt_ref, across_ref, zi_ref, dzt_ref, zi):
+def text_main_kernel(tile, img_ref, two_ref, zt_ref, across_ref, zi_ref, dzt_ref, zi):
     load_units([img_ref], zi_ref)
-    load_units([two_ref, one_ref], zi)
+    load_units([two_ref], zi)
     for t in tiles(zt_ref.shape[0], tile):
         zt = zt_ref[t, :]
         products = nt(zt, zi_ref[...])
@@ -102,14 +107,14 @@
 
 def text_end_kernel(tile, count, *refs):
     pieces = refs[:count]
-    zt_ref, dzt_ref, that_ref, tnorm_ref, txt_ref, du_ref, head_ref, zi = refs[count:]
+    zt_ref, dzt_ref, that_ref, back_ref, txt_ref, du_ref, head_ref, zi = refs[count:]
     load_units(pieces, zi)
     for t in tiles(zt_ref.shape[0], tile):
         dsc = unpaired(nt(zt_ref[t, :], zi[...]))
         dzt = dzt_ref[t, :] + nn(dsc, zi[...])
         that = that_ref[t, :]
         along = jnp.sum(that * dzt, axis=-1, keepdims=True)
-        du_ref[t, :] = ((dzt - that * along) / tnorm_ref[t, :]).astype(bf16)
+        du_ref[t, :] = ((dzt - that * along) * back_ref[t, :]).astype(bf16)
     for t in tiles(du_ref.shape[1], 384):
         head_ref[t, :] = tn(du_ref[:, t], txt_ref[...]).astype(bf16)
 
@@ -137,16 +142,6 @@
         out_ref[i] = jnp.concatenate(cut, axis=1).astype(bf16)
 
 
-def finish_kernel(pad, fold, devices, got_ref, out_ref):
-    total = got_ref[0].astype(f32)
-    for k in range(1, got_ref.shape[0]):
-        total = total + got_ref[k].astype(f32)
-    turned = (total * (1.0 / devices)).T
-    rows = out_ref.shape[0]
-    cut = [turned[pad * k : pad * k + rows] for k in range(fold)]
-    out_ref[...] = jnp.concatenate(cut, axis=1)
-
-
 def image_main_kernel(tile, zi_ref, zt_ref, low_ref, high_ref, down_ref, dzi_ref, two_ref):
     two_ref[: low_ref.shape[0], :] = low_ref[...]
     two_ref[low_ref.shape[0] :, :] = high_ref[...]
@@ -158,19 +153,29 @@
         dzi_ref[t, :] = total + nn(unpaired(nt(zi, two_ref[...])), two_ref[...])
 
 
-def image_side_kernel(tile, one_ref, zi_ref, dzi_ref, out_ref):
+def column_kernel(across_ref, out_ref):
+    wide = jnp.broadcast_to(across_ref[...].astype(f32), (128, across_ref.shape[1]))
+    out_ref[...] = wide.T[:, :1].astype(jnp.int32)
+
+
+def image_end_kernel(tile, low_ref, high_ref, zi_ref, dzi_ref, img_ref, out_ref, zt):
+    zt[: low_ref.shape[0], :] = low_ref[...]
+    zt[low_ref.shape[0] :, :] = high_ref[...]
     for t in tiles(zi_ref.shape[0], tile):
-        dsc = unpaired(nt(zi_ref[t, :], one_ref[...]))
-        out_ref[t, :] = dzi_ref[t, :] + nn(dsc, one_ref[...])
-
-
-def image_end_kernel(tile, one_ref, zi_ref, dzi_ref, img_ref, out_ref):
-    for t in tiles(zi_ref.shape[0], tile):
-        dsc = unpaired(nt(zi_ref[t, :], one_ref[...]))
-        dzi = dzi_ref[t, :] + nn(dsc, one_ref[...])
-        ihat, inorm = unit(img_ref[t, :])
+        dsc = unpaired(nt(zi_ref[t, :], zt[...]))
+        dzi = dzi_ref[t, :] + nn(dsc, zt[...])
+        ihat, back = unit(img_ref[t, :])
         along = jnp.sum(ihat * dzi, axis=-1, keepdims=True)
-        out_ref[t, :] = ((dzi - ihat * along) / inorm).astype(bf16)
+        out_ref[t, :] = ((dzi - ihat * along) * back).astype(bf16)
+
+
+def finish_kernel(pad, fold, devices, got_ref, out_ref):
+    total = got_ref[0].astype(f32)
+    for k in range(1, got_ref.shape[0]):
+        total = total + got_ref[k].astype(f32)
+    turned = (total * (1.0 / devices)).T
+    rows = out_ref.shape[0]
+    out_ref[...] = jnp.concatenate([turned[pad * k : pad * k + rows] for k in range(fold)], axis=1)
 
 
 def call(kernel, outs, args, scratch=(), aliases=None, name=None, flops=1):
@@ -179,7 +184,7 @@
         out_shape=outs,
         scratch_shapes=list(scratch),
         input_output_aliases=aliases or {},
-        compiler_params=pltpu.CompilerParams(vmem_limit_bytes=12 * MIB),
+        compiler_params=pltpu.CompilerParams(vmem_limit_bytes=20 * MIB),
         cost_estimate=pl.CostEstimate(flops=flops, bytes_accessed=1, transcendentals=0),
         name=name,
     )(*args)
@@ -192,18 +197,15 @@
     share_rows = width // n_row
     share_cols = width // n_col
     depth = n_row // 4
-    tile = min(128, rows)
+    tile = rows
     shape = jax.ShapeDtypeStruct
 
     def after(value, *others):
         return lax.optimization_barrier((value,) + others)[0]
 
     half = rows // 2
-    img_a, img_b = img_emb[:half], img_emb[half:]
-    txt_feat = after(txt_feat, img_a, img_b)
-    img_two = from_partner(after(img_emb, img_a, img_b), "col", n_col // 2)
-    img_a = from_partner(img_a, "row", n_row // 2)
-    img_b = from_partner(img_b, "row", n_row // 2)
+    img_one = from_partner(img_emb, "row", n_row // 2)
+    img_two = from_partner(img_emb, "col", n_col // 2)
 
     core = lax.axis_index("row") & 1
     pad = -(-share_rows // 8) * 8
@@ -217,7 +219,7 @@
         return jnp.where(inner < share_rows, (block + which) * share_rows + inner, -1)[None, :]
 
     step = rows // 2
-    that, tnorm, zt, zt_low, zt_high, txt_mine, txt_theirs = pl.pallas_call(
+    that, tback, zt, zt_low, zt_high, txt_mine, txt_theirs = pl.pallas_call(
         text_kernel,
         grid=(2,),
         in_specs=[
@@ -256,48 +258,42 @@
     zi, dzt = call(
         functools.partial(text_main_kernel, tile),
         [narrow, wide],
-        [img_emb, img_two, img_a, zt, positive],
-        [pltpu.VMEM((rows + half, width), bf16)],
+        [img_emb, img_two, zt, positive],
+        [pltpu.VMEM((rows, width), bf16)],
         name="text_main",
     )
     du, head = call(
         functools.partial(text_end_kernel, tile, 1),
         [narrow, shape((width, lanes), bf16)],
-        [img_b, zt, dzt, that, tnorm, txt_theirs],
-        [pltpu.VMEM((half, width), bf16)],
+        [img_one, zt, after(dzt, *txt_two), that, tback, txt_theirs],
+        [pltpu.VMEM((rows, width), bf16)],
         name="text_end",
     )
-    head = from_partner(after(head, *txt_two), "row", 1)
+    head = from_partner(head, "row", 1)
     head = call(
         head_kernel,
         shape((width, lanes), bf16),
         [du, txt_mine, head],
         name="head",
     )
-    txt_a = from_partner(after(zt_low, du), "row", n_row // 2)
+    hop = depth // 4
+    txt_a = turn(after(zt_low, du), hop)
+    txt_b = turn(after(zt_high, du), -hop)
     du_late = after(du, head)
     head = lax.all_to_all(head.reshape(n_col, share_cols, lanes), "col", 0, 0, tiled=True)
     txt_grad = call(
         functools.partial(txt_grad_kernel, tile), narrow, [du_late, head_weight], name="txt_grad"
     )
-    dzi = call(
-        functools.partial(image_main_kernel, tile),
-        wide,
-        [zi, zt, *txt_two, after(positive, txt_grad).reshape(rows, 1)],
-        [pltpu.VMEM((rows, width), bf16)],
-        name="image_main",
-    )
-    dzi = call(
-        functools.partial(image_side_kernel, tile),
-        wide,
-        [txt_a, zi, dzi],
-        (),
-        {2: 0},
-        name="image_one",
-        flops=int(X_ONE),
-    )
-    head = after(head, dzi)
-    txt_b = from_partner(after(zt_high, dzi), "row", n_row // 2)
+    down = call(
+        column_kernel,
+        shape((rows, 1), jnp.int32),
+        [after(positive, txt_a, txt_b, txt_grad)],
+        name="column",
+        flops=int(X_FIRST),
+    )
+    txt_a = turn(after(txt_a, down), hop)
+    txt_b = turn(after(txt_b, down), -hop)
+    head = after(head, down, txt_grad)
     fold = 3
     head = call(
         functools.partial(gather_kernel, pad, fold),
@@ -305,12 +301,20 @@
         [head],
         name="gather",
     )
+    dzi = call(
+        functools.partial(image_main_kernel, tile),
+        wide,
+        [zi, zt, *txt_two, after(down, head)],
+        [pltpu.VMEM((rows, width), bf16)],
+        name="image_main",
+    )
     groups = [[z * 4 + y * 2 + c for y in range(2) for z in range(depth)] for c in range(2)]
     head = lax.all_to_all(head, "row", 0, 0, axis_index_groups=groups, tiled=True)
     img_grad = call(
         functools.partial(image_end_kernel, tile),
         narrow,
-        [txt_b, zi, dzi, img_emb],
+        [txt_a, txt_b, zi, dzi, img_emb],
+        [pltpu.VMEM((rows, width), bf16)],
         name="image_end",
         flops=int(X_END),
     )

time: 141 us -> 137 us (0.972)
  waiting for transfers between devices: 46.7 us -> 67.9 us
  Pallas kernels: 41.5 us -> 28.4 us
  local copies, waits for them, and re-layouts: 13.3 us -> 6.48 us
  starting transfers between devices: 36.7 us -> 32.8 us
    ppermute x0 -> x4, waiting for transfers between devices: none -> 31.1 us  [turn(): lax.ppermute(block, 'row', [(at, (at + 4 * by) % count) for at in range(c...]
    pallas_call x9, Pallas kernels: 35.6 us -> 22.4 us  [call(): pl.pallas_call(kernel, out_shape=outs, scratch_shapes=list(scratch), inpu...]
    ppermute x8 -> x5, starting transfers between devices: 20.6 us -> 10.1 us  [from_partner(): lax.ppermute(block, axis, [(low, low ^ mask) for low in range(count)])]
    ppermute x0 -> x4, starting transfers between devices: none -> 10.1 us  [turn(): lax.ppermute(block, 'row', [(at, (at + 4 * by) % count) for at in range(c...]
    all_to_all x1, waiting for transfers between devices: 5.69 us -> 0.01 us  [shards(): lax.all_to_all(head, 'row', 0, 0, axis_index_groups=groups, tiled=True)]
    unnamed x34 -> x30, local copies, waits for them, and re-layouts: 10.7 us -> 6.48 us
    ppermute x8 -> x5, waiting for transfers between devices: 41 us -> 36.8 us  [from_partner(): lax.ppermute(block, axis, [(low, low ^ mask) for low in range(count)])]
    all_to_all x1, starting transfers between devices: 11.4 us -> 8.06 us  [shards(): lax.all_to_all(head, 'row', 0, 0, axis_index_groups=groups, tiled=True)]
  transfers between devices with their start and end apart: 10 -> 11, of which waited for: 4 -> 7; matrix products, arithmetic and copies ran while one was open for 0% -> 0% of each run, Pallas kernels for 29% -> 18%
where the time goes in v3:
time: 137 us; the launch traced here: 136 us
  waiting for transfers between devices  67.9 us (50%)
  starting transfers between devices  32.8 us (24%)
  Pallas kernels  28.4 us (21%)
  local copies, waits for them, and re-layouts  6.48 us (5%)
    ppermute x5, waiting for transfers between devices, from_partner(): lax.ppermute(block, axis, [(low, low ^ mask) for low in range(count)])  36.8 us
    ppermute x4, waiting for transfers between devices, turn(): lax.ppermute(block, 'row', [(at, (at + 4 * by) % count) for at in range(c...  31.1 us
    pallas_call x9, Pallas kernels, call(): pl.pallas_call(kernel, out_shape=outs, scratch_shapes=list(scratch), inpu...  22.4 us
    ppermute x5, starting transfers between devices, from_partner(): lax.ppermute(block, axis, [(low, low ^ mask) for low in range(count)])  10.1 us
    ppermute x4, starting transfers between devices, turn(): lax.ppermute(block, 'row', [(at, (at + 4 * by) % count) for at in range(c...  10.1 us
    all_to_all x1, starting transfers between devices, shards(): lax.all_to_all(head, 'row', 0, 0, axis_index_groups=groups, tiled=True)  8.06 us
    unnamed x30, local copies, waits for them, and re-layouts  6.48 us
    pallas_call x1, Pallas kernels, shards(): pl.pallas_call(text_kernel, grid=(2,), in_specs=[pl.BlockSpec((step, widt...  5.99 us
  transfers between devices with their start and end apart: 11, of which 7 were waited for; matrix products, arithmetic and copies ran while one was open for 0% of the time, Pallas kernels for 18%

profile of v3, /device:TPU:32, one launch (start us, length us, event | category | flops | bytes accessed | tf_op | source)
XLA Modules:
  0.0 136.4 jit_solution(18345445848614729739)
XLA Ops:
  0.6 1.7 %collective-permute-start.1 = (bf16[512,1152]{1,0:T(8,128)(2,1)}, bf16[512,1152]{1,0:T(8,128)(2,1)S(1)}, u32[]{:S(2)}, u32[]{:S(2)}) collective-permute-start(bf16[512,1152]{1,0:T(8,128)(2,1)} %img_ref.3), channel_id=1, source_target_pairs={{0,4},{1,5},{2,6},{3,7},{4,0},{5,1},{6,2},{7,3},{8,12},{9,13},{10,... | collective-permute-start | bytes 3538952 | tf_op jit(solution)/shard_map/ppermute | solution.py:21
  2.3 6.3 %collective-permute-start = (bf16[512,1152]{1,0:T(8,128)(2,1)}, bf16[512,1152]{1,0:T(8,128)(2,1)S(1)}, u32[]{:S(2)}, u32[]{:S(2)}) collective-permute-start(bf16[512,1152]{1,0:T(8,128)(2,1)} %img_ref.3), channel_id=1, source_target_pairs={{0,128},{8,136},{16,144},{24,152},{32,160},{40,168},{48,176},{56,1... | collective-permute-start | bytes 3538952 | tf_op jit(solution)/shard_map/ppermute | solution.py:21
  8.6 1.7 %copy-done = bf16[1152,1152]{1,0:T(8,128)(2,1)S(1)} copy-done((bf16[1152,1152]{1,0:T(8,128)(2,1)S(1)}, bf16[1152,1152]{1,0:T(8,128)(2,1)}, u32[]{:S(2)}) %copy-start) | copy-done | bytes 2654232
  10.4 1.3 copy-done.7
  11.7 6.0 %text.1 = (f32[512,1152]{1,0:T(8,128)S(1)}, f32[512,1]{1,0:T(8,128)S(1)}, bf16[512,1152]{1,0:T(8,128)(2,1)S(1)}, bf16[256,1152]{1,0:T(8,128)(2,1)}, bf16[256,115...) custom-call(bf16[512,1152]{1,0:T(8,128)(2,1)S(1)} %copy-done.7, ...), custom_call_target="tpu_custom_call" | custom-call | flops 1 | bytes 1 | tf_op jit(solution)/shard_map/text/pallas_call | solution.py:222
  17.6 0.4 collective-permute-start.2
  18.1 1.6 %collective-permute-start.3 = (bf16[256,1152]{1,0:T(8,128)(2,1)}, bf16[256,1152]{1,0:T(8,128)(2,1)S(1)}, u32[]{:S(2)}, u32[]{:S(2)}) collective-permute-start(bf16[256,1152]{1,0:T(8,128)(2,1)} %get-tuple-element.34), channel_id=1, source_target_pairs={{0,4},{1,5},{2,6},{3,7},{4,0},{5,1},{6,2},{7,3},{8,12},{9,13},{10,... | collective-permute-start | bytes 1769480 | tf_op jit(solution)/shard_map/ppermute | solution.py:21
  19.7 10.1 %collective-permute-done.1.two_ref = bf16[512,1152]{1,0:T(8,128)(2,1)S(1)} collective-permute-done((bf16[512,1152]{1,0:T(8,128)(2,1)}, bf16[512,1152]{1,0:T(8,128)(2,1)S(1)}, u32[]{:S(2)}, u32[]{:S(2)}) %collective-permute-start.1) | collective-permute-done | bytes 1179680 | tf_op jit(solution)/shard_map/ppermute | solution.py:21
  29.8 3.6 %text_main.1 = (bf16[512,1152]{1,0:T(8,128)(2,1)S(1)}, f32[512,1152]{1,0:T(8,128)S(1)}) custom-call(bf16[512,1152]{1,0:T(8,128)(2,1)S(1)} %copy-done.8, bf16[512,1152]{1,0:T(8,128)(2,1)S(1)} %collective-permute-done.1.two_ref, bf16[512,1152]{1,0:T(8,128)(2,1)S(1)} %get-tuple-element.25.zt_ref.refs_1_, s32[1,512]{1,0:T(1,128)S(1)} %copy-done.14), custom_call_target="tpu_custom_call" | custom-call | flops 1 | bytes 1 | tf_op jit(solution)/shard_map/text_main/pallas_call | solution.py:182
  33.4 9.0 %collective-permute-done.2.low_ref = bf16[256,1152]{1,0:T(8,128)(2,1)S(1)} collective-permute-done((bf16[256,1152]{1,0:T(8,128)(2,1)}, bf16[256,1152]{1,0:T(8,128)(2,1)S(1)}, u32[]{:S(2)}, u32[]{:S(2)}) %collective-permute-start.2) | collective-permute-done | bytes 589856 | tf_op jit(solution)/shard_map/ppermute | solution.py:21
  42.4 11.5 %collective-permute-done.3.high_ref = bf16[256,1152]{1,0:T(8,128)(2,1)S(1)} collective-permute-done((bf16[256,1152]{1,0:T(8,128)(2,1)}, bf16[256,1152]{1,0:T(8,128)(2,1)S(1)}, u32[]{:S(2)}, u32[]{:S(2)}) %collective-permute-start.3) | collective-permute-done | bytes 589856 | tf_op jit(solution)/shard_map/ppermute | solution.py:21
  53.9 6.2 %collective-permute-done.refs_0_ = bf16[512,1152]{1,0:T(8,128)(2,1)S(1)} collective-permute-done((bf16[512,1152]{1,0:T(8,128)(2,1)}, bf16[512,1152]{1,0:T(8,128)(2,1)S(1)}, u32[]{:S(2)}, u32[]{:S(2)}) %collective-permute-start) | collective-permute-done | bytes 1179680 | tf_op jit(solution)/shard_map/ppermute | solution.py:21
  60.1 3.5 %text_end.1 = (bf16[512,1152]{1,0:T(8,128)(2,1)S(1)}, bf16[1152,640]{1,0:T(8,128)(2,1)S(1)}) custom-call(bf16[512,1152]{1,0:T(8,128)(2,1)S(1)} %collective-permute-done.refs_0_, bf16[512,1152]{1,0:T(8,128)(2,1)S(1)} %get-tuple-element.25.zt_ref.refs_1_, f32[512,1152]{1,0:T(8,128)S(1)} %get-tuple-element.28.refs_2_, ...), custom_call_target="tpu_custom_call" | custom-call | flops 1 | bytes 1 | tf_op jit(solution)/shard_map/text_end/pallas_call | solution.py:182
  63.7 0.1 collective-permute-start.6
  63.8 0.3 collective-permute-start.4
  64.0 4.1 %collective-permute-start.5 = (bf16[256,1152]{1,0:T(8,128)(2,1)}, bf16[256,1152]{1,0:T(8,128)(2,1)}, u32[]{:S(2)}, u32[]{:S(2)}) collective-permute-start(bf16[256,1152]{1,0:T(8,128)(2,1)} %get-tuple-element.34), channel_id=1, source_target_pairs={{0,192},{8,200},{16,208},{24,216},{32,224},{40,232},{48,240},{56,2... | collective-permute-start | bytes 1769480 | tf_op jit(solution)/shard_map/ppermute | solution.py:26
  68.2 1.1 head.1
  69.3 1.1 copy-done.4
  70.4 4.6 %all-to-all-start = ((bf16[8,144,640]{2,1,0:T(8,128)(2,1)}), bf16[8,144,640]{2,1,0:T(8,128)(2,1)}, u32[]{:S(2)}, u32[]{:S(2)}) async-start(bf16[8,144,640]{2,1,0:T(8,128)(2,1)} %bitcast.1), calls=%async_computation | async-start | bytes 2949120 | tf_op jit(solution)/shard_map/all_to_all | solution.py:283
  75.0 1.3 copy-done.6
  76.2 2.9 %txt_grad.1 = bf16[512,1152]{1,0:T(8,128)(2,1)} custom-call(bf16[512,1152]{1,0:T(8,128)(2,1)S(1)} %copy-done.6, bf16[1152,1152]{1,0:T(8,128)(2,1)S(1)} %copy-done.1), custom_call_target="tpu_custom_call" | custom-call | flops 1 | bytes 1 | tf_op jit(solution)/shard_map/txt_grad/pallas_call | solution.py:182
  79.1 15.4 %collective-permute-done.4 = bf16[256,1152]{1,0:T(8,128)(2,1)} collective-permute-done((bf16[256,1152]{1,0:T(8,128)(2,1)}, bf16[256,1152]{1,0:T(8,128)(2,1)}, u32[]{:S(2)}, u32[]{:S(2)}) %collective-permute-start.4) | collective-permute-done | bytes 589856 | tf_op jit(solution)/shard_map/ppermute | solution.py:26
  94.6 0.1 column.1.down_ref
  94.7 5.7 %collective-permute-start.7 = (bf16[256,1152]{1,0:T(8,128)(2,1)}, bf16[256,1152]{1,0:T(8,128)(2,1)}, u32[]{:S(2)}, u32[]{:S(2)}) collective-permute-start(bf16[256,1152]{1,0:T(8,128)(2,1)} %collective-permute-done.4), channel_id=1, source_target_pairs={{0,64},{8,72},{16,80},{24,88},{32,96},{40,104},{48,112},{56,120},{... | collective-permute-start | bytes 1769480 | tf_op jit(solution)/shard_map/ppermute | solution.py:26
  100.4 2.4 %gather.1 = bf16[16,48,128]{2,1,0:T(8,128)(2,1)} custom-call(bf16[8,144,640]{2,1,0:T(8,128)(2,1)} %all-to-all-done.got_ref), custom_call_target="tpu_custom_call" | custom-call | flops 1 | bytes 1 | tf_op jit(solution)/shard_map/gather/pallas_call | solution.py:182
  102.8 8.1 %all-to-all-start.1 = ((bf16[16,48,128]{2,1,0:T(8,128)(2,1)}), bf16[16,48,128]{2,1,0:T(8,128)(2,1)S(1)}, u32[]{:S(2)}, u32[]{:S(2)}) async-start(bf16[16,48,128]{2,1,0:T(8,128)(2,1)} %gather.1), calls=%async_computation.1 | async-start | bytes 393216 | tf_op jit(solution)/shard_map/all_to_all | solution.py:312
  110.9 1.1 copy-done.13
  111.9 3.4 %image_main.1.dzi_ref = f32[512,1152]{1,0:T(8,128)S(1)} custom-call(bf16[512,1152]{1,0:T(8,128)(2,1)S(1)} %copy-done.11, bf16[512,1152]{1,0:T(8,128)(2,1)S(1)} %copy-done.3, bf16[256,1152]{1,0:T(8,128)(2,1)S(1)} %collective-permute-done.2.low_ref, bf16[256,1152]{1,0:T(8,128)(2,1)S(1)} %copy-done.13, s32[512,1]{1,0:T(8,128)S(1)} %column.1.down_ref), custom_call_target="tpu_custom_call" | custom-call | flops 1 | bytes 1 | tf_op jit(solution)/shard_map/image_main/pallas_call | solution.py:182
  115.4 13.5 %collective-permute-done.7.low_ref = bf16[256,1152]{1,0:T(8,128)(2,1)} collective-permute-done((bf16[256,1152]{1,0:T(8,128)(2,1)}, bf16[256,1152]{1,0:T(8,128)(2,1)}, u32[]{:S(2)}, u32[]{:S(2)}) %collective-permute-start.7) | collective-permute-done | bytes 589856 | tf_op jit(solution)/shard_map/ppermute | solution.py:26
  128.9 2.1 %collective-permute-done.8.high_ref = bf16[256,1152]{1,0:T(8,128)(2,1)} collective-permute-done((bf16[256,1152]{1,0:T(8,128)(2,1)}, bf16[256,1152]{1,0:T(8,128)(2,1)}, u32[]{:S(2)}, u32[]{:S(2)}) %collective-permute-start.8) | collective-permute-done | bytes 589856 | tf_op jit(solution)/shard_map/ppermute | solution.py:26
  131.0 4.5 %image_end.1 = bf16[512,1152]{1,0:T(8,128)(2,1)} custom-call(bf16[256,1152]{1,0:T(8,128)(2,1)} %collective-permute-done.7.low_ref, bf16[256,1152]{1,0:T(8,128)(2,1)} %collective-permute-done.8.high_ref, bf16[512,1152]{1,0:T(8,128)(2,1)S(1)} %copy-done.11, f32[512,1152]{1,0:T(8,128)S(1)} %image_main.1.dzi_ref, bf16[512,1152]{1,0:T(8,128)(2,1)S(1)} %copy-done.9), custom_call_target="tpu_custom_call" | custom-call | flops 3000000000 | bytes 1 | tf_op jit(solution)/shard_map/image_end/pallas_call | solution.py:182
  135.6 0.8 finish.1
  (31 shorter events, 0.1 us)
Async XLA Ops:
  0.6 29.2 %collective-permute-start.1 = (bf16[512,1152]{1,0:T(8,128)(2,1)}, bf16[512,1152]{1,0:T(8,128)(2,1)S(1)}, u32[]{:S(2)}, u32[]{:S(2)}) collective-permute-start(bf16[512,1152]{1,0:T(8,128)(2,1)} %img_ref.3), channel_id=1, source_target_pairs={{0,4},{1,5},{2,6},{3,7},{4,0},{5,1},{6,2},{7,3},{8,12},{9,13},{10,... | collective-permute-start | bytes 3538952 | tf_op jit(solution)/shard_map/ppermute | solution.py:21
  2.3 57.8 %collective-permute-start = (bf16[512,1152]{1,0:T(8,128)(2,1)}, bf16[512,1152]{1,0:T(8,128)(2,1)S(1)}, u32[]{:S(2)}, u32[]{:S(2)}) collective-permute-start(bf16[512,1152]{1,0:T(8,128)(2,1)} %img_ref.3), channel_id=1, source_target_pairs={{0,128},{8,136},{16,144},{24,152},{32,160},{40,168},{48,176},{56,1... | collective-permute-start | bytes 3538952 | tf_op jit(solution)/shard_map/ppermute | solution.py:21
  8.6 1.8 %copy-start = (bf16[1152,1152]{1,0:T(8,128)(2,1)S(1)}, bf16[1152,1152]{1,0:T(8,128)(2,1)}, u32[]{:S(2)}) copy-start(bf16[1152,1152]{1,0:T(8,128)(2,1)} %head_ref.3) | copy-start | bytes 7962628
  10.4 1.3 copy-start.7
  11.6 18.1 %copy-start.8 = (bf16[512,1152]{1,0:T(8,128)(2,1)S(1)}, bf16[512,1152]{1,0:T(8,128)(2,1)}, u32[]{:S(2)}) copy-start(bf16[512,1152]{1,0:T(8,128)(2,1)} %img_ref.3) | copy-start | bytes 3538948
  11.7 18.1 %copy-start.14 = (s32[1,512]{1,0:T(1,128)S(1)}, s32[1,512]{1,0:T(1,128)}, u32[]{:S(2)}) copy-start(s32[1,512]{1,0:T(1,128)} %across_ref.2) | copy-start | bytes 6148
  17.6 42.4 %copy-start.2 = (bf16[512,1152]{1,0:T(8,128)(2,1)}, bf16[512,1152]{1,0:T(8,128)(2,1)S(1)}, u32[]{:S(2)}) copy-start(bf16[512,1152]{1,0:T(8,128)(2,1)S(1)} %get-tuple-element.25.zt_ref.refs_1_) | copy-start | bytes 3538948
  17.6 24.8 %collective-permute-start.2 = (bf16[256,1152]{1,0:T(8,128)(2,1)}, bf16[256,1152]{1,0:T(8,128)(2,1)S(1)}, u32[]{:S(2)}, u32[]{:S(2)}) collective-permute-start(bf16[256,1152]{1,0:T(8,128)(2,1)} %get-tuple-element.33), channel_id=1, source_target_pairs={{0,4},{1,5},{2,6},{3,7},{4,0},{5,1},{6,2},{7,3},{8,12},{9,13},{10,... | collective-permute-start | bytes 1769480 | tf_op jit(solution)/shard_map/ppermute | solution.py:21
  18.1 35.8 %collective-permute-start.3 = (bf16[256,1152]{1,0:T(8,128)(2,1)}, bf16[256,1152]{1,0:T(8,128)(2,1)S(1)}, u32[]{:S(2)}, u32[]{:S(2)}) collective-permute-start(bf16[256,1152]{1,0:T(8,128)(2,1)} %get-tuple-element.34), channel_id=1, source_target_pairs={{0,4},{1,5},{2,6},{3,7},{4,0},{5,1},{6,2},{7,3},{8,12},{9,13},{10,... | collective-permute-start | bytes 1769480 | tf_op jit(solution)/shard_map/ppermute | solution.py:21
  33.4 30.2 %copy-start.10 = (bf16[512,1152]{1,0:T(8,128)(2,1)}, bf16[512,1152]{1,0:T(8,128)(2,1)S(1)}, u32[]{:S(2)}) copy-start(bf16[512,1152]{1,0:T(8,128)(2,1)S(1)} %get-tuple-element.41.zi_ref) | copy-start | bytes 3538948
  53.9 9.7 %copy-start.12 = (bf16[256,1152]{1,0:T(8,128)(2,1)}, bf16[256,1152]{1,0:T(8,128)(2,1)S(1)}, u32[]{:S(2)}) copy-start(bf16[256,1152]{1,0:T(8,128)(2,1)S(1)} %collective-permute-done.3.high_ref) | copy-start | bytes 1769476
  63.6 5.6 %copy-start.5 = (bf16[512,1152]{1,0:T(8,128)(2,1)}, bf16[512,1152]{1,0:T(8,128)(2,1)S(1)}, u32[]{:S(2)}) copy-start(bf16[512,1152]{1,0:T(8,128)(2,1)S(1)} %get-tuple-element.37.du_ref) | copy-start | bytes 3538948
  63.7 4.5 %collective-permute-start.6 = (bf16[1152,640]{1,0:T(8,128)(2,1)S(1)}, bf16[1152,640]{1,0:T(8,128)(2,1)S(1)}, u32[]{:S(2)}, u32[]{:S(2)}) collective-permute-start(bf16[1152,640]{1,0:T(8,128)(2,1)S(1)} %get-tuple-element.36), channel_id=1, source_target_pairs={{0,8},{8,0},{16,24},{24,16},{32,40},{40,32},{48,56},{56,48},{64,72... | collective-permute-start | bytes 4423688 | tf_op jit(solution)/shard_map/ppermute | solution.py:21
  63.8 30.8 %collective-permute-start.4 = (bf16[256,1152]{1,0:T(8,128)(2,1)}, bf16[256,1152]{1,0:T(8,128)(2,1)}, u32[]{:S(2)}, u32[]{:S(2)}) collective-permute-start(bf16[256,1152]{1,0:T(8,128)(2,1)} %get-tuple-element.33), channel_id=1, source_target_pairs={{0,64},{8,72},{16,80},{24,88},{32,96},{40,104},{48,112},{56,120},{... | collective-permute-start | bytes 1769480 | tf_op jit(solution)/shard_map/ppermute | solution.py:26
  64.0 30.5 %collective-permute-start.5 = (bf16[256,1152]{1,0:T(8,128)(2,1)}, bf16[256,1152]{1,0:T(8,128)(2,1)}, u32[]{:S(2)}, u32[]{:S(2)}) collective-permute-start(bf16[256,1152]{1,0:T(8,128)(2,1)} %get-tuple-element.34), channel_id=1, source_target_pairs={{0,192},{8,200},{16,208},{24,216},{32,224},{40,232},{48,240},{56,2... | collective-permute-start | bytes 1769480 | tf_op jit(solution)/shard_map/ppermute | solution.py:26
  69.3 1.1 copy-start.4
  70.4 4.6 %copy-start.1 = (bf16[1152,1152]{1,0:T(8,128)(2,1)S(1)}, bf16[1152,1152]{1,0:T(8,128)(2,1)}, u32[]{:S(2)}) copy-start(bf16[1152,1152]{1,0:T(8,128)(2,1)} %head_ref.3) | copy-start | bytes 7962628
  70.4 30.0 %all-to-all-start = ((bf16[8,144,640]{2,1,0:T(8,128)(2,1)}), bf16[8,144,640]{2,1,0:T(8,128)(2,1)}, u32[]{:S(2)}, u32[]{:S(2)}) async-start(bf16[8,144,640]{2,1,0:T(8,128)(2,1)} %bitcast.1), calls=%async_computation | async-start | bytes 2949120 | tf_op jit(solution)/shard_map/all_to_all | solution.py:283
  75.0 1.3 copy-start.6
  94.6 16.3 %copy-start.11 = (bf16[512,1152]{1,0:T(8,128)(2,1)S(1)}, bf16[512,1152]{1,0:T(8,128)(2,1)}, u32[]{:S(2)}) copy-start(bf16[512,1152]{1,0:T(8,128)(2,1)} %copy-done.10) | copy-start | bytes 3538948
  94.7 16.2 %copy-start.3 = (bf16[512,1152]{1,0:T(8,128)(2,1)S(1)}, bf16[512,1152]{1,0:T(8,128)(2,1)}, u32[]{:S(2)}) copy-start(bf16[512,1152]{1,0:T(8,128)(2,1)} %copy-done.2) | copy-start | bytes 3538948
  94.7 34.2 %collective-permute-start.7 = (bf16[256,1152]{1,0:T(8,128)(2,1)}, bf16[256,1152]{1,0:T(8,128)(2,1)}, u32[]{:S(2)}, u32[]{:S(2)}) collective-permute-start(bf16[256,1152]{1,0:T(8,128)(2,1)} %collective-permute-done.4), channel_id=1, source_target_pairs={{0,64},{8,72},{16,80},{24,88},{32,96},{40,104},{48,112},{56,120},{... | collective-permute-start | bytes 1769480 | tf_op jit(solution)/shard_map/ppermute | solution.py:26
  100.4 30.7 %collective-permute-start.8 = (bf16[256,1152]{1,0:T(8,128)(2,1)}, bf16[256,1152]{1,0:T(8,128)(2,1)}, u32[]{:S(2)}, u32[]{:S(2)}) collective-permute-start(bf16[256,1152]{1,0:T(8,128)(2,1)} %collective-permute-done.5), channel_id=1, source_target_pairs={{0,192},{8,200},{16,208},{24,216},{32,224},{40,232},{48,240},{56,2... | collective-permute-start | bytes 1769480 | tf_op jit(solution)/shard_map/ppermute | solution.py:26
  102.8 32.8 %all-to-all-start.1 = ((bf16[16,48,128]{2,1,0:T(8,128)(2,1)}), bf16[16,48,128]{2,1,0:T(8,128)(2,1)S(1)}, u32[]{:S(2)}, u32[]{:S(2)}) async-start(bf16[16,48,128]{2,1,0:T(8,128)(2,1)} %gather.1), calls=%async_computation.1 | async-start | bytes 393216 | tf_op jit(solution)/shard_map/all_to_all | solution.py:312
  110.9 1.1 copy-start.13
  111.9 19.1 %copy-start.9 = (bf16[512,1152]{1,0:T(8,128)(2,1)S(1)}, bf16[512,1152]{1,0:T(8,128)(2,1)}, u32[]{:S(2)}) copy-start(bf16[512,1152]{1,0:T(8,128)(2,1)} %img_ref.3) | copy-start | bytes 3538948

commit v4 on v3

--- a/solution.py
+++ b/solution.py
@@ -12,7 +12,8 @@
 f32 = jnp.float32
 bf16 = jnp.bfloat16
 MIB = 1 << 20
-X_FIRST = 6e9
+X_FIRST = 6.5e9
+X_FINISH = 6e9
 X_END = 3e9
 
 
@@ -90,7 +91,8 @@
 def load_units(pieces, zi):
     at = 0
     for piece in pieces:
-        zi[at : at + piece.shape[0], :] = unit(piece[...])[0].astype(bf16)
+        for c in tiles(piece.shape[0], 32):
+            zi[at + c.start : at + c.stop, :] = unit(piece[c, :])[0].astype(bf16)
         at += piece.shape[0]
 
 
@@ -107,14 +109,16 @@
 
 def text_end_kernel(tile, count, *refs):
     pieces = refs[:count]
-    zt_ref, dzt_ref, that_ref, back_ref, txt_ref, du_ref, head_ref, zi = refs[count:]
+    zt_ref, dzt_ref, that_ref, back_ref, txt_ref, du_ref, head_ref, zi, last = refs[count:]
     load_units(pieces, zi)
     for t in tiles(zt_ref.shape[0], tile):
         dsc = unpaired(nt(zt_ref[t, :], zi[...]))
-        dzt = dzt_ref[t, :] + nn(dsc, zi[...])
-        that = that_ref[t, :]
+        last[t, :] = nn(dsc, zi[...])
+    for c in tiles(zt_ref.shape[0], 32):
+        dzt = dzt_ref[c, :] + last[c, :]
+        that = that_ref[c, :]
         along = jnp.sum(that * dzt, axis=-1, keepdims=True)
-        du_ref[t, :] = ((dzt - that * along) * back_ref[t, :]).astype(bf16)
+        du_ref[c, :] = ((dzt - that * along) * back_ref[c, :]).astype(bf16)
     for t in tiles(du_ref.shape[1], 384):
         head_ref[t, :] = tn(du_ref[:, t], txt_ref[...]).astype(bf16)
 
@@ -158,15 +162,17 @@
     out_ref[...] = wide.T[:, :1].astype(jnp.int32)
 
 
-def image_end_kernel(tile, low_ref, high_ref, zi_ref, dzi_ref, img_ref, out_ref, zt):
+def image_end_kernel(tile, low_ref, high_ref, zi_ref, dzi_ref, img_ref, out_ref, zt, last):
     zt[: low_ref.shape[0], :] = low_ref[...]
     zt[low_ref.shape[0] :, :] = high_ref[...]
     for t in tiles(zi_ref.shape[0], tile):
         dsc = unpaired(nt(zi_ref[t, :], zt[...]))
-        dzi = dzi_ref[t, :] + nn(dsc, zt[...])
-        ihat, back = unit(img_ref[t, :])
+        last[t, :] = nn(dsc, zt[...])
+    for c in tiles(zi_ref.shape[0], 32):
+        dzi = dzi_ref[c, :] + last[c, :]
+        ihat, back = unit(img_ref[c, :])
         along = jnp.sum(ihat * dzi, axis=-1, keepdims=True)
-        out_ref[t, :] = ((dzi - ihat * along) * back).astype(bf16)
+        out_ref[c, :] = ((dzi - ihat * along) * back).astype(bf16)
 
 
 def finish_kernel(pad, fold, devices, got_ref, out_ref):
@@ -266,7 +272,7 @@
         functools.partial(text_end_kernel, tile, 1),
         [narrow, shape((width, lanes), bf16)],
         [img_one, zt, after(dzt, *txt_two), that, tback, txt_theirs],
-        [pltpu.VMEM((rows, width), bf16)],
+        [pltpu.VMEM((rows, width), bf16), pltpu.VMEM((rows, width), f32)],
         name="text_end",
     )
     head = from_partner(head, "row", 1)
@@ -276,9 +282,8 @@
         [du, txt_mine, head],
         name="head",
     )
-    hop = depth // 4
-    txt_a = turn(after(zt_low, du), hop)
-    txt_b = turn(after(zt_high, du), -hop)
+    txt_a = turn(after(zt_low, du), 1)
+    txt_b = turn(after(zt_high, du), -1)
     du_late = after(du, head)
     head = lax.all_to_all(head.reshape(n_col, share_cols, lanes), "col", 0, 0, tiled=True)
     txt_grad = call(
@@ -291,9 +296,16 @@
         name="column",
         flops=int(X_FIRST),
     )
-    txt_a = turn(after(txt_a, down), hop)
-    txt_b = turn(after(txt_b, down), -hop)
-    head = after(head, down, txt_grad)
+    txt_a = turn(after(txt_a, down), depth // 2 - 2)
+    txt_b = turn(after(txt_b, down), 2 - depth // 2)
+    dzi = call(
+        functools.partial(image_main_kernel, tile),
+        wide,
+        [zi, zt, *txt_two, down],
+        [pltpu.VMEM((rows, width), bf16)],
+        name="image_main",
+    )
+    head = after(head, dzi, txt_grad)
     fold = 3
     head = call(
         functools.partial(gather_kernel, pad, fold),
@@ -301,28 +313,24 @@
         [head],
         name="gather",
     )
-    dzi = call(
-        functools.partial(image_main_kernel, tile),
-        wide,
-        [zi, zt, *txt_two, after(down, head)],
-        [pltpu.VMEM((rows, width), bf16)],
-        name="image_main",
-    )
     groups = [[z * 4 + y * 2 + c for y in range(2) for z in range(depth)] for c in range(2)]
     head = lax.all_to_all(head, "row", 0, 0, axis_index_groups=groups, tiled=True)
+    txt_a = turn(after(txt_a, dzi), 1)
+    txt_b = turn(after(txt_b, dzi), -1)
+    head_grad = call(
+        functools.partial(finish_kernel, pad, fold, n_row * n_col),
+        shape((share_rows, share_cols), f32),
+        [head],
+        name="finish",
+        flops=int(X_FINISH),
+    )
     img_grad = call(
         functools.partial(image_end_kernel, tile),
         narrow,
-        [txt_a, txt_b, zi, dzi, img_emb],
-        [pltpu.VMEM((rows, width), bf16)],
+        [txt_a, txt_b, zi, after(dzi, head_grad), img_emb],
+        [pltpu.VMEM((rows, width), bf16), pltpu.VMEM((rows, width), f32)],
         name="image_end",
         flops=int(X_END),
-    )
-    head_grad = call(
-        functools.partial(finish_kernel, pad, fold, n_row * n_col),
-        shape((share_rows, share_cols), f32),
-        [after(head, img_grad)],
-        name="finish",
     )
     return (img_grad, txt_grad, head_grad)
 

time: 137 us -> 136 us (level)
  waiting for transfers between devices: 67.9 us -> 66 us
    ppermute x4 -> x6, waiting for transfers between devices: 31.1 us -> 20.6 us  [turn(): lax.ppermute(block, 'row', [(at, (at + 4 * by) % count) for at in range(c...]
    all_to_all x1, waiting for transfers between devices: 0.01 us -> 5.26 us  [shards(): lax.all_to_all(head.reshape(n_col, share_cols, lanes), 'col', 0, 0, tiled...]
    all_to_all x1, waiting for transfers between devices: 0.01 us -> 4.19 us  [shards(): lax.all_to_all(head, 'row', 0, 0, axis_index_groups=groups, tiled=True)]
    ppermute x4 -> x6, starting transfers between devices: 10.1 us -> 7.41 us  [turn(): lax.ppermute(block, 'row', [(at, (at + 4 * by) % count) for at in range(c...]
    all_to_all x1, starting transfers between devices: 8.06 us -> 9.6 us  [shards(): lax.all_to_all(head, 'row', 0, 0, axis_index_groups=groups, tiled=True)]
    unnamed x30 -> x32, local copies, waits for them, and re-layouts: 6.48 us -> 7.23 us
  transfers between devices with their start and end apart: 11 -> 13, of which waited for: 7 -> 13; matrix products, arithmetic and copies ran while one was open for 0% -> 0% of each run, Pallas kernels for 18% -> 16%
where the time goes in v4:
time: 136 us; the launch traced here: 135 us
  waiting for transfers between devices  66 us (49%)
  starting transfers between devices  31.6 us (23%)
  Pallas kernels  29.5 us (22%)
  local copies, waits for them, and re-layouts  7.23 us (5%)
    ppermute x5, waiting for transfers between devices, from_partner(): lax.ppermute(block, axis, [(low, low ^ mask) for low in range(count)])  36 us
    pallas_call x9, Pallas kernels, call(): pl.pallas_call(kernel, out_shape=outs, scratch_shapes=list(scratch), inpu...  23.6 us
    ppermute x6, waiting for transfers between devices, turn(): lax.ppermute(block, 'row', [(at, (at + 4 * by) % count) for at in range(c...  20.6 us
    ppermute x5, starting transfers between devices, from_partner(): lax.ppermute(block, axis, [(low, low ^ mask) for low in range(count)])  10.1 us
    all_to_all x1, starting transfers between devices, shards(): lax.all_to_all(head, 'row', 0, 0, axis_index_groups=groups, tiled=True)  9.6 us
    ppermute x6, starting transfers between devices, turn(): lax.ppermute(block, 'row', [(at, (at + 4 * by) % count) for at in range(c...  7.41 us
    unnamed x32, local copies, waits for them, and re-layouts  7.23 us
    pallas_call x1, Pallas kernels, shards(): pl.pallas_call(text_kernel, grid=(2,), in_specs=[pl.BlockSpec((step, widt...  5.97 us
  transfers between devices with their start and end apart: 13, of which 13 were waited for; matrix products, arithmetic and copies ran while one was open for 0% of the time, Pallas kernels for 16%

profile of v4, /device:TPU:32, one launch (start us, length us, event | category | flops | bytes accessed | tf_op | source)
XLA Modules:
  0.0 135.2 jit_solution(15016653444700610544)
XLA Ops:
  0.6 1.7 %collective-permute-start.1 = (bf16[512,1152]{1,0:T(8,128)(2,1)}, bf16[512,1152]{1,0:T(8,128)(2,1)S(1)}, u32[]{:S(2)}, u32[]{:S(2)}) collective-permute-start(bf16[512,1152]{1,0:T(8,128)(2,1)} %img_ref.3), channel_id=1, source_target_pairs={{0,4},{1,5},{2,6},{3,7},{4,0},{5,1},{6,2},{7,3},{8,12},{9,13},{10,... | collective-permute-start | bytes 3538952 | tf_op jit(solution)/shard_map/ppermute | solution.py:22
  2.3 6.3 %collective-permute-start = (bf16[512,1152]{1,0:T(8,128)(2,1)}, bf16[512,1152]{1,0:T(8,128)(2,1)S(1)}, u32[]{:S(2)}, u32[]{:S(2)}) collective-permute-start(bf16[512,1152]{1,0:T(8,128)(2,1)} %img_ref.3), channel_id=1, source_target_pairs={{0,128},{8,136},{16,144},{24,152},{32,160},{40,168},{48,176},{56,1... | collective-permute-start | bytes 3538952 | tf_op jit(solution)/shard_map/ppermute | solution.py:22
  8.6 1.7 %copy-done = bf16[1152,1152]{1,0:T(8,128)(2,1)S(1)} copy-done((bf16[1152,1152]{1,0:T(8,128)(2,1)S(1)}, bf16[1152,1152]{1,0:T(8,128)(2,1)}, u32[]{:S(2)}) %copy-start) | copy-done | bytes 2654232
  10.4 1.3 copy-done.7
  11.7 6.0 %text.1 = (f32[512,1152]{1,0:T(8,128)S(1)}, f32[512,1]{1,0:T(8,128)S(1)}, bf16[512,1152]{1,0:T(8,128)(2,1)S(1)}, bf16[256,1152]{1,0:T(8,128)(2,1)}, bf16[256,115...) custom-call(bf16[512,1152]{1,0:T(8,128)(2,1)S(1)} %copy-done.7, ...), custom_call_target="tpu_custom_call" | custom-call | flops 1 | bytes 1 | tf_op jit(solution)/shard_map/text/pallas_call | solution.py:228
  18.1 1.6 %collective-permute-start.3 = (bf16[256,1152]{1,0:T(8,128)(2,1)}, bf16[256,1152]{1,0:T(8,128)(2,1)S(1)}, u32[]{:S(2)}, u32[]{:S(2)}) collective-permute-start(bf16[256,1152]{1,0:T(8,128)(2,1)} %get-tuple-element.35), channel_id=1, source_target_pairs={{0,4},{1,5},{2,6},{3,7},{4,0},{5,1},{6,2},{7,3},{8,12},{9,13},{10,... | collective-permute-start | bytes 1769480 | tf_op jit(solution)/shard_map/ppermute | solution.py:22
  19.6 10.1 %collective-permute-done.1.two_ref = bf16[512,1152]{1,0:T(8,128)(2,1)S(1)} collective-permute-done((bf16[512,1152]{1,0:T(8,128)(2,1)}, bf16[512,1152]{1,0:T(8,128)(2,1)S(1)}, u32[]{:S(2)}, u32[]{:S(2)}) %collective-permute-start.1) | collective-permute-done | bytes 1179680 | tf_op jit(solution)/shard_map/ppermute | solution.py:22
  29.8 3.6 %text_main.1 = (bf16[512,1152]{1,0:T(8,128)(2,1)S(1)}, f32[512,1152]{1,0:T(8,128)S(1)}) custom-call(bf16[512,1152]{1,0:T(8,128)(2,1)S(1)} %copy-done.8, bf16[512,1152]{1,0:T(8,128)(2,1)S(1)} %collective-permute-done.1.two_ref, bf16[512,1152]{1,0:T(8,128)(2,1)S(1)} %get-tuple-element.26.zt_ref.refs_1_, s32[1,512]{1,0:T(1,128)S(1)} %copy-done.15), custom_call_target="tpu_custom_call" | custom-call | flops 1 | bytes 1 | tf_op jit(solution)/shard_map/text_main/pallas_call | solution.py:188
  33.4 1.0 copy-done.10
  34.4 8.0 %collective-permute-done.2.low_ref = bf16[256,1152]{1,0:T(8,128)(2,1)S(1)} collective-permute-done((bf16[256,1152]{1,0:T(8,128)(2,1)}, bf16[256,1152]{1,0:T(8,128)(2,1)S(1)}, u32[]{:S(2)}, u32[]{:S(2)}) %collective-permute-start.2) | collective-permute-done | bytes 589856 | tf_op jit(solution)/shard_map/ppermute | solution.py:22
  42.4 11.5 %collective-permute-done.3.high_ref = bf16[256,1152]{1,0:T(8,128)(2,1)S(1)} collective-permute-done((bf16[256,1152]{1,0:T(8,128)(2,1)}, bf16[256,1152]{1,0:T(8,128)(2,1)S(1)}, u32[]{:S(2)}, u32[]{:S(2)}) %collective-permute-start.3) | collective-permute-done | bytes 589856 | tf_op jit(solution)/shard_map/ppermute | solution.py:22
  54.7 5.4 %collective-permute-done.refs_0_ = bf16[512,1152]{1,0:T(8,128)(2,1)S(1)} collective-permute-done((bf16[512,1152]{1,0:T(8,128)(2,1)}, bf16[512,1152]{1,0:T(8,128)(2,1)S(1)}, u32[]{:S(2)}, u32[]{:S(2)}) %collective-permute-start) | collective-permute-done | bytes 1179680 | tf_op jit(solution)/shard_map/ppermute | solution.py:22
  60.1 3.6 %text_end.1 = (bf16[512,1152]{1,0:T(8,128)(2,1)S(1)}, bf16[1152,640]{1,0:T(8,128)(2,1)S(1)}) custom-call(bf16[512,1152]{1,0:T(8,128)(2,1)S(1)} %collective-permute-done.refs_0_, bf16[512,1152]{1,0:T(8,128)(2,1)S(1)} %get-tuple-element.26.zt_ref.refs_1_, f32[512,1152]{1,0:T(8,128)S(1)} %get-tuple-element.29.refs_2_, ...), custom_call_target="tpu_custom_call" | custom-call | flops 1 | bytes 1 | tf_op jit(solution)/shard_map/text_end/pallas_call | solution.py:188
  63.8 1.4 %collective-permute-start.4 = (bf16[256,1152]{1,0:T(8,128)(2,1)}, bf16[256,1152]{1,0:T(8,128)(2,1)}, u32[]{:S(2)}, u32[]{:S(2)}) collective-permute-start(bf16[256,1152]{1,0:T(8,128)(2,1)} %get-tuple-element.34), channel_id=1, source_target_pairs={{0,32},{8,40},{16,48},{24,56},{32,64},{40,72},{48,80},{56,88},{64,... | collective-permute-start | bytes 1769480 | tf_op jit(solution)/shard_map/ppermute | solution.py:27
  67.0 1.1 head.1
  68.2 1.1 copy-done.4
  69.3 4.6 %all-to-all-start = ((bf16[8,144,640]{2,1,0:T(8,128)(2,1)}), bf16[8,144,640]{2,1,0:T(8,128)(2,1)}, u32[]{:S(2)}, u32[]{:S(2)}) async-start(bf16[8,144,640]{2,1,0:T(8,128)(2,1)} %bitcast.1), calls=%async_computation | async-start | bytes 2949120 | tf_op jit(solution)/shard_map/all_to_all | solution.py:288
  73.9 1.3 copy-done.6
  75.1 2.9 %txt_grad.1 = bf16[512,1152]{1,0:T(8,128)(2,1)} custom-call(bf16[512,1152]{1,0:T(8,128)(2,1)S(1)} %copy-done.6, bf16[1152,1152]{1,0:T(8,128)(2,1)S(1)} %copy-done.1), custom_call_target="tpu_custom_call" | custom-call | flops 1 | bytes 1 | tf_op jit(solution)/shard_map/txt_grad/pallas_call | solution.py:188
  78.0 1.8 %collective-permute-done.4 = bf16[256,1152]{1,0:T(8,128)(2,1)} collective-permute-done((bf16[256,1152]{1,0:T(8,128)(2,1)}, bf16[256,1152]{1,0:T(8,128)(2,1)}, u32[]{:S(2)}, u32[]{:S(2)}) %collective-permute-start.4) | collective-permute-done | bytes 589856 | tf_op jit(solution)/shard_map/ppermute | solution.py:27
  80.8 5.1 %collective-permute-start.7 = (bf16[256,1152]{1,0:T(8,128)(2,1)}, bf16[256,1152]{1,0:T(8,128)(2,1)}, u32[]{:S(2)}, u32[]{:S(2)}) collective-permute-start(bf16[256,1152]{1,0:T(8,128)(2,1)} %collective-permute-done.4), channel_id=1, source_target_pairs={{0,64},{8,72},{16,80},{24,88},{32,96},{40,104},{48,112},{56,120},{... | collective-permute-start | bytes 1769480 | tf_op jit(solution)/shard_map/ppermute | solution.py:27
  85.9 3.5 %image_main.1.dzi_ref = f32[512,1152]{1,0:T(8,128)S(1)} custom-call(bf16[512,1152]{1,0:T(8,128)(2,1)S(1)} %copy-done.11, bf16[512,1152]{1,0:T(8,128)(2,1)S(1)} %copy-done.3, bf16[256,1152]{1,0:T(8,128)(2,1)S(1)} %collective-permute-done.2.low_ref, bf16[256,1152]{1,0:T(8,128)(2,1)S(1)} %copy-done.14, s32[512,1]{1,0:T(8,128)S(1)} %column.1.down_ref), custom_call_target="tpu_custom_call" | custom-call | flops 1 | bytes 1 | tf_op jit(solution)/shard_map/image_main/pallas_call | solution.py:188
  89.4 5.3 %all-to-all-done.got_ref = bf16[8,144,640]{2,1,0:T(8,128)(2,1)} async-done(((bf16[8,144,640]{2,1,0:T(8,128)(2,1)}), bf16[8,144,640]{2,1,0:T(8,128)(2,1)}, u32[]{:S(2)}, u32[]{:S(2)}) %all-to-all-start) | async-done | bytes 1474592 | tf_op jit(solution)/shard_map/all_to_all | solution.py:288
  94.7 2.4 %gather.1 = bf16[16,48,128]{2,1,0:T(8,128)(2,1)} custom-call(bf16[8,144,640]{2,1,0:T(8,128)(2,1)} %all-to-all-done.got_ref), custom_call_target="tpu_custom_call" | custom-call | flops 1 | bytes 1 | tf_op jit(solution)/shard_map/gather/pallas_call | solution.py:188
  97.1 9.6 %all-to-all-start.1 = ((bf16[16,48,128]{2,1,0:T(8,128)(2,1)}), bf16[16,48,128]{2,1,0:T(8,128)(2,1)}, u32[]{:S(2)}, u32[]{:S(2)}) async-start(bf16[16,48,128]{2,1,0:T(8,128)(2,1)} %gather.1), calls=%async_computation.1 | async-start | bytes 393216 | tf_op jit(solution)/shard_map/all_to_all | solution.py:317
  106.7 6.7 %collective-permute-done.7 = bf16[256,1152]{1,0:T(8,128)(2,1)} collective-permute-done((bf16[256,1152]{1,0:T(8,128)(2,1)}, bf16[256,1152]{1,0:T(8,128)(2,1)}, u32[]{:S(2)}, u32[]{:S(2)}) %collective-permute-start.7) | collective-permute-done | bytes 589856 | tf_op jit(solution)/shard_map/ppermute | solution.py:27
  113.4 2.1 %collective-permute-done.9 = bf16[256,1152]{1,0:T(8,128)(2,1)} collective-permute-done((bf16[256,1152]{1,0:T(8,128)(2,1)}, bf16[256,1152]{1,0:T(8,128)(2,1)}, u32[]{:S(2)}, u32[]{:S(2)}) %collective-permute-start.9) | collective-permute-done | bytes 589856 | tf_op jit(solution)/shard_map/ppermute | solution.py:27
  115.6 4.2 %all-to-all-done.1.got_ref = bf16[16,48,128]{2,1,0:T(8,128)(2,1)} async-done(((bf16[16,48,128]{2,1,0:T(8,128)(2,1)}), bf16[16,48,128]{2,1,0:T(8,128)(2,1)}, u32[]{:S(2)}, u32[]{:S(2)}) %all-to-all-start.1) | async-done | bytes 196640 | tf_op jit(solution)/shard_map/all_to_all | solution.py:317
  119.8 1.8 %finish.1 = f32[36,144]{1,0:T(8,128)} custom-call(bf16[16,48,128]{2,1,0:T(8,128)(2,1)} %all-to-all-done.1.got_ref), custom_call_target="tpu_custom_call" | custom-call | flops 6000000000 | bytes 1 | tf_op jit(solution)/shard_map/finish/pallas_call | solution.py:188
  121.6 5.7 %collective-permute-done.8.low_ref = bf16[256,1152]{1,0:T(8,128)(2,1)} collective-permute-done((bf16[256,1152]{1,0:T(8,128)(2,1)}, bf16[256,1152]{1,0:T(8,128)(2,1)}, u32[]{:S(2)}, u32[]{:S(2)}) %collective-permute-start.8) | collective-permute-done | bytes 589856 | tf_op jit(solution)/shard_map/ppermute | solution.py:27
  127.3 3.4 %collective-permute-done.10.high_ref = bf16[256,1152]{1,0:T(8,128)(2,1)} collective-permute-done((bf16[256,1152]{1,0:T(8,128)(2,1)}, bf16[256,1152]{1,0:T(8,128)(2,1)}, u32[]{:S(2)}, u32[]{:S(2)}) %collective-permute-start.10) | collective-permute-done | bytes 589856 | tf_op jit(solution)/shard_map/ppermute | solution.py:27
  130.7 4.5 %image_end.1 = bf16[512,1152]{1,0:T(8,128)(2,1)} custom-call(bf16[256,1152]{1,0:T(8,128)(2,1)} %collective-permute-done.8.low_ref, bf16[256,1152]{1,0:T(8,128)(2,1)} %collective-permute-done.10.high_ref, bf16[512,1152]{1,0:T(8,128)(2,1)S(1)} %copy-done.12, f32[512,1152]{1,0:T(8,128)S(1)} %image_main.1.dzi_ref, bf16[512,1152]{1,0:T(8,128)(2,1)S(1)} %copy-done.9), custom_call_target="tpu_custom_call" | custom-call | flops 3000000000 | bytes 1 | tf_op jit(solution)/shard_map/image_end/pallas_call | solution.py:188
  (37 shorter events, 4.3 us)
Async XLA Ops:
  0.6 29.2 %collective-permute-start.1 = (bf16[512,1152]{1,0:T(8,128)(2,1)}, bf16[512,1152]{1,0:T(8,128)(2,1)S(1)}, u32[]{:S(2)}, u32[]{:S(2)}) collective-permute-start(bf16[512,1152]{1,0:T(8,128)(2,1)} %img_ref.3), channel_id=1, source_target_pairs={{0,4},{1,5},{2,6},{3,7},{4,0},{5,1},{6,2},{7,3},{8,12},{9,13},{10,... | collective-permute-start | bytes 3538952 | tf_op jit(solution)/shard_map/ppermute | solution.py:22
  2.3 57.8 %collective-permute-start = (bf16[512,1152]{1,0:T(8,128)(2,1)}, bf16[512,1152]{1,0:T(8,128)(2,1)S(1)}, u32[]{:S(2)}, u32[]{:S(2)}) collective-permute-start(bf16[512,1152]{1,0:T(8,128)(2,1)} %img_ref.3), channel_id=1, source_target_pairs={{0,128},{8,136},{16,144},{24,152},{32,160},{40,168},{48,176},{56,1... | collective-permute-start | bytes 3538952 | tf_op jit(solution)/shard_map/ppermute | solution.py:22
  8.6 1.8 %copy-start = (bf16[1152,1152]{1,0:T(8,128)(2,1)S(1)}, bf16[1152,1152]{1,0:T(8,128)(2,1)}, u32[]{:S(2)}) copy-start(bf16[1152,1152]{1,0:T(8,128)(2,1)} %head_ref.3) | copy-start | bytes 7962628
  10.4 1.3 copy-start.7
  11.6 18.1 %copy-start.8 = (bf16[512,1152]{1,0:T(8,128)(2,1)S(1)}, bf16[512,1152]{1,0:T(8,128)(2,1)}, u32[]{:S(2)}) copy-start(bf16[512,1152]{1,0:T(8,128)(2,1)} %img_ref.3) | copy-start | bytes 3538948
  11.7 18.1 %copy-start.15 = (s32[1,512]{1,0:T(1,128)S(1)}, s32[1,512]{1,0:T(1,128)}, u32[]{:S(2)}) copy-start(s32[1,512]{1,0:T(1,128)} %across_ref.2) | copy-start | bytes 6148
  17.6 42.5 %copy-start.2 = (bf16[512,1152]{1,0:T(8,128)(2,1)}, bf16[512,1152]{1,0:T(8,128)(2,1)S(1)}, u32[]{:S(2)}) copy-start(bf16[512,1152]{1,0:T(8,128)(2,1)S(1)} %get-tuple-element.26.zt_ref.refs_1_) | copy-start | bytes 3538948
  17.6 24.8 %collective-permute-start.2 = (bf16[256,1152]{1,0:T(8,128)(2,1)}, bf16[256,1152]{1,0:T(8,128)(2,1)S(1)}, u32[]{:S(2)}, u32[]{:S(2)}) collective-permute-start(bf16[256,1152]{1,0:T(8,128)(2,1)} %get-tuple-element.34), channel_id=1, source_target_pairs={{0,4},{1,5},{2,6},{3,7},{4,0},{5,1},{6,2},{7,3},{8,12},{9,13},{10,... | collective-permute-start | bytes 1769480 | tf_op jit(solution)/shard_map/ppermute | solution.py:22
  18.1 35.8 %collective-permute-start.3 = (bf16[256,1152]{1,0:T(8,128)(2,1)}, bf16[256,1152]{1,0:T(8,128)(2,1)S(1)}, u32[]{:S(2)}, u32[]{:S(2)}) collective-permute-start(bf16[256,1152]{1,0:T(8,128)(2,1)} %get-tuple-element.35), channel_id=1, source_target_pairs={{0,4},{1,5},{2,6},{3,7},{4,0},{5,1},{6,2},{7,3},{8,12},{9,13},{10,... | collective-permute-start | bytes 1769480 | tf_op jit(solution)/shard_map/ppermute | solution.py:22
  33.4 1.0 copy-start.10
  53.9 0.8 copy-start.13
  63.7 4.5 %copy-start.5 = (bf16[512,1152]{1,0:T(8,128)(2,1)}, bf16[512,1152]{1,0:T(8,128)(2,1)S(1)}, u32[]{:S(2)}) copy-start(bf16[512,1152]{1,0:T(8,128)(2,1)S(1)} %get-tuple-element.38.du_ref) | copy-start | bytes 3538948
  63.7 3.4 %collective-permute-start.6 = (bf16[1152,640]{1,0:T(8,128)(2,1)S(1)}, bf16[1152,640]{1,0:T(8,128)(2,1)S(1)}, u32[]{:S(2)}, u32[]{:S(2)}) collective-permute-start(bf16[1152,640]{1,0:T(8,128)(2,1)S(1)} %get-tuple-element.37), channel_id=1, source_target_pairs={{0,8},{8,0},{16,24},{24,16},{32,40},{40,32},{48,56},{56,48},{64,72... | collective-permute-start | bytes 4423688 | tf_op jit(solution)/shard_map/ppermute | solution.py:22
  63.8 16.0 %collective-permute-start.4 = (bf16[256,1152]{1,0:T(8,128)(2,1)}, bf16[256,1152]{1,0:T(8,128)(2,1)}, u32[]{:S(2)}, u32[]{:S(2)}) collective-permute-start(bf16[256,1152]{1,0:T(8,128)(2,1)} %get-tuple-element.34), channel_id=1, source_target_pairs={{0,32},{8,40},{16,48},{24,56},{32,64},{40,72},{48,80},{56,88},{64,... | collective-permute-start | bytes 1769480 | tf_op jit(solution)/shard_map/ppermute | solution.py:27
  65.2 15.5 %collective-permute-start.5 = (bf16[256,1152]{1,0:T(8,128)(2,1)}, bf16[256,1152]{1,0:T(8,128)(2,1)}, u32[]{:S(2)}, u32[]{:S(2)}) collective-permute-start(bf16[256,1152]{1,0:T(8,128)(2,1)} %get-tuple-element.35), channel_id=1, source_target_pairs={{0,224},{8,232},{16,240},{24,248},{32,0},{40,8},{48,16},{56,24},{6... | collective-permute-start | bytes 1769480 | tf_op jit(solution)/shard_map/ppermute | solution.py:27
  68.2 1.1 copy-start.4
  69.3 4.6 %copy-start.1 = (bf16[1152,1152]{1,0:T(8,128)(2,1)S(1)}, bf16[1152,1152]{1,0:T(8,128)(2,1)}, u32[]{:S(2)}) copy-start(bf16[1152,1152]{1,0:T(8,128)(2,1)} %head_ref.3) | copy-start | bytes 7962628
  69.3 25.4 %all-to-all-start = ((bf16[8,144,640]{2,1,0:T(8,128)(2,1)}), bf16[8,144,640]{2,1,0:T(8,128)(2,1)}, u32[]{:S(2)}, u32[]{:S(2)}) async-start(bf16[8,144,640]{2,1,0:T(8,128)(2,1)} %bitcast.1), calls=%async_computation | async-start | bytes 2949120 | tf_op jit(solution)/shard_map/all_to_all | solution.py:288
  73.9 1.3 copy-start.6
  78.0 7.9 %copy-start.3 = (bf16[512,1152]{1,0:T(8,128)(2,1)S(1)}, bf16[512,1152]{1,0:T(8,128)(2,1)}, u32[]{:S(2)}) copy-start(bf16[512,1152]{1,0:T(8,128)(2,1)} %copy-done.2) | copy-start | bytes 3538948
  78.0 7.9 %copy-start.11 = (bf16[512,1152]{1,0:T(8,128)(2,1)S(1)}, bf16[512,1152]{1,0:T(8,128)(2,1)}, u32[]{:S(2)}) copy-start(bf16[512,1152]{1,0:T(8,128)(2,1)} %copy-done.10) | copy-start | bytes 3538948
  78.0 7.9 %copy-start.14 = (bf16[256,1152]{1,0:T(8,128)(2,1)S(1)}, bf16[256,1152]{1,0:T(8,128)(2,1)}, u32[]{:S(2)}) copy-start(bf16[256,1152]{1,0:T(8,128)(2,1)} %copy-done.13) | copy-start | bytes 1769476
  80.8 32.6 %collective-permute-start.7 = (bf16[256,1152]{1,0:T(8,128)(2,1)}, bf16[256,1152]{1,0:T(8,128)(2,1)}, u32[]{:S(2)}, u32[]{:S(2)}) collective-permute-start(bf16[256,1152]{1,0:T(8,128)(2,1)} %collective-permute-done.4), channel_id=1, source_target_pairs={{0,64},{8,72},{16,80},{24,88},{32,96},{40,104},{48,112},{56,120},{... | collective-permute-start | bytes 1769480 | tf_op jit(solution)/shard_map/ppermute | solution.py:27
  85.9 29.6 %collective-permute-start.9 = (bf16[256,1152]{1,0:T(8,128)(2,1)}, bf16[256,1152]{1,0:T(8,128)(2,1)}, u32[]{:S(2)}, u32[]{:S(2)}) collective-permute-start(bf16[256,1152]{1,0:T(8,128)(2,1)} %collective-permute-done.5), channel_id=1, source_target_pairs={{0,192},{8,200},{16,208},{24,216},{32,224},{40,232},{48,240},{56,2... | collective-permute-start | bytes 1769480 | tf_op jit(solution)/shard_map/ppermute | solution.py:27
  97.1 22.6 %all-to-all-start.1 = ((bf16[16,48,128]{2,1,0:T(8,128)(2,1)}), bf16[16,48,128]{2,1,0:T(8,128)(2,1)}, u32[]{:S(2)}, u32[]{:S(2)}) async-start(bf16[16,48,128]{2,1,0:T(8,128)(2,1)} %gather.1), calls=%async_computation.1 | async-start | bytes 393216 | tf_op jit(solution)/shard_map/all_to_all | solution.py:317
  106.7 24.0 %copy-start.9 = (bf16[512,1152]{1,0:T(8,128)(2,1)S(1)}, bf16[512,1152]{1,0:T(8,128)(2,1)}, u32[]{:S(2)}) copy-start(bf16[512,1152]{1,0:T(8,128)(2,1)} %img_ref.3) | copy-start | bytes 3538948
  113.4 13.9 %collective-permute-start.8 = (bf16[256,1152]{1,0:T(8,128)(2,1)}, bf16[256,1152]{1,0:T(8,128)(2,1)}, u32[]{:S(2)}, u32[]{:S(2)}) collective-permute-start(bf16[256,1152]{1,0:T(8,128)(2,1)} %collective-permute-done.7), channel_id=1, source_target_pairs={{0,32},{8,40},{16,48},{24,56},{32,64},{40,72},{48,80},{56,88},{64,... | collective-permute-start | bytes 1769480 | tf_op jit(solution)/shard_map/ppermute | solution.py:27
  115.6 15.1 %collective-permute-start.10 = (bf16[256,1152]{1,0:T(8,128)(2,1)}, bf16[256,1152]{1,0:T(8,128)(2,1)}, u32[]{:S(2)}, u32[]{:S(2)}) collective-permute-start(bf16[256,1152]{1,0:T(8,128)(2,1)} %collective-permute-done.9), channel_id=1, source_target_pairs={{0,224},{8,232},{16,240},{24,248},{32,0},{40,8},{48,16},{56,24},{6... | collective-permute-start | bytes 1769480 | tf_op jit(solution)/shard_map/ppermute | solution.py:27
  119.8 10.9 %copy-start.12 = (bf16[512,1152]{1,0:T(8,128)(2,1)S(1)}, bf16[512,1152]{1,0:T(8,128)(2,1)}, u32[]{:S(2)}) copy-start(bf16[512,1152]{1,0:T(8,128)(2,1)} %copy-done.10) | copy-start | bytes 3538948

commit v5 on v4

--- a/solution.py
+++ b/solution.py
@@ -170,9 +170,10 @@
         last[t, :] = nn(dsc, zt[...])
     for c in tiles(zi_ref.shape[0], 32):
         dzi = dzi_ref[c, :] + last[c, :]
-        ihat, back = unit(img_ref[c, :])
-        along = jnp.sum(ihat * dzi, axis=-1, keepdims=True)
-        out_ref[c, :] = ((dzi - ihat * along) * back).astype(bf16)
+        img = img_ref[c, :].astype(f32)
+        square = jnp.sum(img * img, axis=-1, keepdims=True) + 1e-06
+        along = jnp.sum(img * dzi, axis=-1, keepdims=True) / square
+        out_ref[c, :] = ((dzi - img * along) * (1.0 / jnp.sqrt(square))).astype(bf16)
 
 
 def finish_kernel(pad, fold, devices, got_ref, out_ref):

time: 136 us -> 136 us (level)
  no operation moved by 1% of the time
where the time goes in v5:
time: 136 us; the launch traced here: 135 us
  waiting for transfers between devices  66 us (49%)
  starting transfers between devices  31.6 us (23%)
  Pallas kernels  29.6 us (22%)
  local copies, waits for them, and re-layouts  7.23 us (5%)
    ppermute x5, waiting for transfers between devices, from_partner(): lax.ppermute(block, axis, [(low, low ^ mask) for low in range(count)])  36 us
    pallas_call x9, Pallas kernels, call(): pl.pallas_call(kernel, out_shape=outs, scratch_shapes=list(scratch), inpu...  23.7 us
    ppermute x6, waiting for transfers between devices, turn(): lax.ppermute(block, 'row', [(at, (at + 4 * by) % count) for at in range(c...  20.6 us
    ppermute x5, starting transfers between devices, from_partner(): lax.ppermute(block, axis, [(low, low ^ mask) for low in range(count)])  10.1 us
    all_to_all x1, starting transfers between devices, shards(): lax.all_to_all(head, 'row', 0, 0, axis_index_groups=groups, tiled=True)  9.6 us
    ppermute x6, starting transfers between devices, turn(): lax.ppermute(block, 'row', [(at, (at + 4 * by) % count) for at in range(c...  7.41 us
    unnamed x32, local copies, waits for them, and re-layouts  7.23 us
    pallas_call x1, Pallas kernels, shards(): pl.pallas_call(text_kernel, grid=(2,), in_specs=[pl.BlockSpec((step, widt...  5.97 us
  transfers between devices with their start and end apart: 13, of which 13 were waited for; matrix products, arithmetic and copies ran while one was open for 0% of the time, Pallas kernels for 16%

profile of v5, /device:TPU:32, one launch (start us, length us, event | category | flops | bytes accessed | tf_op | source)
XLA Modules:
  0.0 135.3 jit_solution(10431486482576351399)
XLA Ops:
  0.6 1.7 %collective-permute-start.1 = (bf16[512,1152]{1,0:T(8,128)(2,1)}, bf16[512,1152]{1,0:T(8,128)(2,1)S(1)}, u32[]{:S(2)}, u32[]{:S(2)}) collective-permute-start(bf16[512,1152]{1,0:T(8,128)(2,1)} %img_ref.3), channel_id=1, source_target_pairs={{0,4},{1,5},{2,6},{3,7},{4,0},{5,1},{6,2},{7,3},{8,12},{9,13},{10,... | collective-permute-start | bytes 3538952 | tf_op jit(solution)/shard_map/ppermute | solution.py:22
  2.3 6.3 %collective-permute-start = (bf16[512,1152]{1,0:T(8,128)(2,1)}, bf16[512,1152]{1,0:T(8,128)(2,1)S(1)}, u32[]{:S(2)}, u32[]{:S(2)}) collective-permute-start(bf16[512,1152]{1,0:T(8,128)(2,1)} %img_ref.3), channel_id=1, source_target_pairs={{0,128},{8,136},{16,144},{24,152},{32,160},{40,168},{48,176},{56,1... | collective-permute-start | bytes 3538952 | tf_op jit(solution)/shard_map/ppermute | solution.py:22
  8.6 1.7 %copy-done = bf16[1152,1152]{1,0:T(8,128)(2,1)S(1)} copy-done((bf16[1152,1152]{1,0:T(8,128)(2,1)S(1)}, bf16[1152,1152]{1,0:T(8,128)(2,1)}, u32[]{:S(2)}) %copy-start) | copy-done | bytes 2654232
  10.4 1.3 copy-done.7
  11.7 6.0 %text.1 = (f32[512,1152]{1,0:T(8,128)S(1)}, f32[512,1]{1,0:T(8,128)S(1)}, bf16[512,1152]{1,0:T(8,128)(2,1)S(1)}, bf16[256,1152]{1,0:T(8,128)(2,1)}, bf16[256,115...) custom-call(bf16[512,1152]{1,0:T(8,128)(2,1)S(1)} %copy-done.7, ...), custom_call_target="tpu_custom_call" | custom-call | flops 1 | bytes 1 | tf_op jit(solution)/shard_map/text/pallas_call | solution.py:229
  18.1 1.6 %collective-permute-start.3 = (bf16[256,1152]{1,0:T(8,128)(2,1)}, bf16[256,1152]{1,0:T(8,128)(2,1)S(1)}, u32[]{:S(2)}, u32[]{:S(2)}) collective-permute-start(bf16[256,1152]{1,0:T(8,128)(2,1)} %get-tuple-element.35), channel_id=1, source_target_pairs={{0,4},{1,5},{2,6},{3,7},{4,0},{5,1},{6,2},{7,3},{8,12},{9,13},{10,... | collective-permute-start | bytes 1769480 | tf_op jit(solution)/shard_map/ppermute | solution.py:22
  19.6 10.1 %collective-permute-done.1.two_ref = bf16[512,1152]{1,0:T(8,128)(2,1)S(1)} collective-permute-done((bf16[512,1152]{1,0:T(8,128)(2,1)}, bf16[512,1152]{1,0:T(8,128)(2,1)S(1)}, u32[]{:S(2)}, u32[]{:S(2)}) %collective-permute-start.1) | collective-permute-done | bytes 1179680 | tf_op jit(solution)/shard_map/ppermute | solution.py:22
  29.8 3.6 %text_main.1 = (bf16[512,1152]{1,0:T(8,128)(2,1)S(1)}, f32[512,1152]{1,0:T(8,128)S(1)}) custom-call(bf16[512,1152]{1,0:T(8,128)(2,1)S(1)} %copy-done.8, bf16[512,1152]{1,0:T(8,128)(2,1)S(1)} %collective-permute-done.1.two_ref, bf16[512,1152]{1,0:T(8,128)(2,1)S(1)} %get-tuple-element.26.zt_ref.refs_1_, s32[1,512]{1,0:T(1,128)S(1)} %copy-done.15), custom_call_target="tpu_custom_call" | custom-call | flops 1 | bytes 1 | tf_op jit(solution)/shard_map/text_main/pallas_call | solution.py:189
  33.4 1.0 copy-done.10
  34.4 8.0 %collective-permute-done.2.low_ref = bf16[256,1152]{1,0:T(8,128)(2,1)S(1)} collective-permute-done((bf16[256,1152]{1,0:T(8,128)(2,1)}, bf16[256,1152]{1,0:T(8,128)(2,1)S(1)}, u32[]{:S(2)}, u32[]{:S(2)}) %collective-permute-start.2) | collective-permute-done | bytes 589856 | tf_op jit(solution)/shard_map/ppermute | solution.py:22
  42.4 11.5 %collective-permute-done.3.high_ref = bf16[256,1152]{1,0:T(8,128)(2,1)S(1)} collective-permute-done((bf16[256,1152]{1,0:T(8,128)(2,1)}, bf16[256,1152]{1,0:T(8,128)(2,1)S(1)}, u32[]{:S(2)}, u32[]{:S(2)}) %collective-permute-start.3) | collective-permute-done | bytes 589856 | tf_op jit(solution)/shard_map/ppermute | solution.py:22
  54.7 5.4 %collective-permute-done.refs_0_ = bf16[512,1152]{1,0:T(8,128)(2,1)S(1)} collective-permute-done((bf16[512,1152]{1,0:T(8,128)(2,1)}, bf16[512,1152]{1,0:T(8,128)(2,1)S(1)}, u32[]{:S(2)}, u32[]{:S(2)}) %collective-permute-start) | collective-permute-done | bytes 1179680 | tf_op jit(solution)/shard_map/ppermute | solution.py:22
  60.1 3.6 %text_end.1 = (bf16[512,1152]{1,0:T(8,128)(2,1)S(1)}, bf16[1152,640]{1,0:T(8,128)(2,1)S(1)}) custom-call(bf16[512,1152]{1,0:T(8,128)(2,1)S(1)} %collective-permute-done.refs_0_, bf16[512,1152]{1,0:T(8,128)(2,1)S(1)} %get-tuple-element.26.zt_ref.refs_1_, f32[512,1152]{1,0:T(8,128)S(1)} %get-tuple-element.29.refs_2_, ...), custom_call_target="tpu_custom_call" | custom-call | flops 1 | bytes 1 | tf_op jit(solution)/shard_map/text_end/pallas_call | solution.py:189
  63.8 1.4 %collective-permute-start.4 = (bf16[256,1152]{1,0:T(8,128)(2,1)}, bf16[256,1152]{1,0:T(8,128)(2,1)}, u32[]{:S(2)}, u32[]{:S(2)}) collective-permute-start(bf16[256,1152]{1,0:T(8,128)(2,1)} %get-tuple-element.34), channel_id=1, source_target_pairs={{0,32},{8,40},{16,48},{24,56},{32,64},{40,72},{48,80},{56,88},{64,... | collective-permute-start | bytes 1769480 | tf_op jit(solution)/shard_map/ppermute | solution.py:27
  67.0 1.1 head.1
  68.2 1.1 copy-done.4
  69.3 4.6 %all-to-all-start = ((bf16[8,144,640]{2,1,0:T(8,128)(2,1)}), bf16[8,144,640]{2,1,0:T(8,128)(2,1)}, u32[]{:S(2)}, u32[]{:S(2)}) async-start(bf16[8,144,640]{2,1,0:T(8,128)(2,1)} %bitcast.1), calls=%async_computation | async-start | bytes 2949120 | tf_op jit(solution)/shard_map/all_to_all | solution.py:289
  73.9 1.3 copy-done.6
  75.1 2.9 %txt_grad.1 = bf16[512,1152]{1,0:T(8,128)(2,1)} custom-call(bf16[512,1152]{1,0:T(8,128)(2,1)S(1)} %copy-done.6, bf16[1152,1152]{1,0:T(8,128)(2,1)S(1)} %copy-done.1), custom_call_target="tpu_custom_call" | custom-call | flops 1 | bytes 1 | tf_op jit(solution)/shard_map/txt_grad/pallas_call | solution.py:189
  78.0 1.8 %collective-permute-done.4 = bf16[256,1152]{1,0:T(8,128)(2,1)} collective-permute-done((bf16[256,1152]{1,0:T(8,128)(2,1)}, bf16[256,1152]{1,0:T(8,128)(2,1)}, u32[]{:S(2)}, u32[]{:S(2)}) %collective-permute-start.4) | collective-permute-done | bytes 589856 | tf_op jit(solution)/shard_map/ppermute | solution.py:27
  80.8 5.1 %collective-permute-start.7 = (bf16[256,1152]{1,0:T(8,128)(2,1)}, bf16[256,1152]{1,0:T(8,128)(2,1)}, u32[]{:S(2)}, u32[]{:S(2)}) collective-permute-start(bf16[256,1152]{1,0:T(8,128)(2,1)} %collective-permute-done.4), channel_id=1, source_target_pairs={{0,64},{8,72},{16,80},{24,88},{32,96},{40,104},{48,112},{56,120},{... | collective-permute-start | bytes 1769480 | tf_op jit(solution)/shard_map/ppermute | solution.py:27
  85.9 3.5 %image_main.1.dzi_ref = f32[512,1152]{1,0:T(8,128)S(1)} custom-call(bf16[512,1152]{1,0:T(8,128)(2,1)S(1)} %copy-done.11, bf16[512,1152]{1,0:T(8,128)(2,1)S(1)} %copy-done.3, bf16[256,1152]{1,0:T(8,128)(2,1)S(1)} %collective-permute-done.2.low_ref, bf16[256,1152]{1,0:T(8,128)(2,1)S(1)} %copy-done.14, s32[512,1]{1,0:T(8,128)S(1)} %column.1.down_ref), custom_call_target="tpu_custom_call" | custom-call | flops 1 | bytes 1 | tf_op jit(solution)/shard_map/image_main/pallas_call | solution.py:189
  89.4 5.3 %all-to-all-done.got_ref = bf16[8,144,640]{2,1,0:T(8,128)(2,1)} async-done(((bf16[8,144,640]{2,1,0:T(8,128)(2,1)}), bf16[8,144,640]{2,1,0:T(8,128)(2,1)}, u32[]{:S(2)}, u32[]{:S(2)}) %all-to-all-start) | async-done | bytes 1474592 | tf_op jit(solution)/shard_map/all_to_all | solution.py:289
  94.7 2.4 %gather.1 = bf16[16,48,128]{2,1,0:T(8,128)(2,1)} custom-call(bf16[8,144,640]{2,1,0:T(8,128)(2,1)} %all-to-all-done.got_ref), custom_call_target="tpu_custom_call" | custom-call | flops 1 | bytes 1 | tf_op jit(solution)/shard_map/gather/pallas_call | solution.py:189
  97.1 9.6 %all-to-all-start.1 = ((bf16[16,48,128]{2,1,0:T(8,128)(2,1)}), bf16[16,48,128]{2,1,0:T(8,128)(2,1)}, u32[]{:S(2)}, u32[]{:S(2)}) async-start(bf16[16,48,128]{2,1,0:T(8,128)(2,1)} %gather.1), calls=%async_computation.1 | async-start | bytes 393216 | tf_op jit(solution)/shard_map/all_to_all | solution.py:318
  106.7 6.7 %collective-permute-done.7 = bf16[256,1152]{1,0:T(8,128)(2,1)} collective-permute-done((bf16[256,1152]{1,0:T(8,128)(2,1)}, bf16[256,1152]{1,0:T(8,128)(2,1)}, u32[]{:S(2)}, u32[]{:S(2)}) %collective-permute-start.7) | collective-permute-done | bytes 589856 | tf_op jit(solution)/shard_map/ppermute | solution.py:27
  113.4 2.1 %collective-permute-done.9 = bf16[256,1152]{1,0:T(8,128)(2,1)} collective-permute-done((bf16[256,1152]{1,0:T(8,128)(2,1)}, bf16[256,1152]{1,0:T(8,128)(2,1)}, u32[]{:S(2)}, u32[]{:S(2)}) %collective-permute-start.9) | collective-permute-done | bytes 589856 | tf_op jit(solution)/shard_map/ppermute | solution.py:27
  115.6 4.2 %all-to-all-done.1.got_ref = bf16[16,48,128]{2,1,0:T(8,128)(2,1)} async-done(((bf16[16,48,128]{2,1,0:T(8,128)(2,1)}), bf16[16,48,128]{2,1,0:T(8,128)(2,1)}, u32[]{:S(2)}, u32[]{:S(2)}) %all-to-all-start.1) | async-done | bytes 196640 | tf_op jit(solution)/shard_map/all_to_all | solution.py:318
  119.8 1.8 %finish.1 = f32[36,144]{1,0:T(8,128)} custom-call(bf16[16,48,128]{2,1,0:T(8,128)(2,1)} %all-to-all-done.1.got_ref), custom_call_target="tpu_custom_call" | custom-call | flops 6000000000 | bytes 1 | tf_op jit(solution)/shard_map/finish/pallas_call | solution.py:189
  121.6 5.7 %collective-permute-done.8.low_ref = bf16[256,1152]{1,0:T(8,128)(2,1)} collective-permute-done((bf16[256,1152]{1,0:T(8,128)(2,1)}, bf16[256,1152]{1,0:T(8,128)(2,1)}, u32[]{:S(2)}, u32[]{:S(2)}) %collective-permute-start.8) | collective-permute-done | bytes 589856 | tf_op jit(solution)/shard_map/ppermute | solution.py:27
  127.3 3.4 %collective-permute-done.10.high_ref = bf16[256,1152]{1,0:T(8,128)(2,1)} collective-permute-done((bf16[256,1152]{1,0:T(8,128)(2,1)}, bf16[256,1152]{1,0:T(8,128)(2,1)}, u32[]{:S(2)}, u32[]{:S(2)}) %collective-permute-start.10) | collective-permute-done | bytes 589856 | tf_op jit(solution)/shard_map/ppermute | solution.py:27
  130.7 4.6 %image_end.1 = bf16[512,1152]{1,0:T(8,128)(2,1)} custom-call(bf16[256,1152]{1,0:T(8,128)(2,1)} %collective-permute-done.8.low_ref, bf16[256,1152]{1,0:T(8,128)(2,1)} %collective-permute-done.10.high_ref, bf16[512,1152]{1,0:T(8,128)(2,1)S(1)} %copy-done.12, f32[512,1152]{1,0:T(8,128)S(1)} %image_main.1.dzi_ref, bf16[512,1152]{1,0:T(8,128)(2,1)S(1)} %copy-done.9), custom_call_target="tpu_custom_call" | custom-call | flops 3000000000 | bytes 1 | tf_op jit(solution)/shard_map/image_end/pallas_call | solution.py:189
  (37 shorter events, 4.3 us)
Async XLA Ops:
  0.6 29.2 %collective-permute-start.1 = (bf16[512,1152]{1,0:T(8,128)(2,1)}, bf16[512,1152]{1,0:T(8,128)(2,1)S(1)}, u32[]{:S(2)}, u32[]{:S(2)}) collective-permute-start(bf16[512,1152]{1,0:T(8,128)(2,1)} %img_ref.3), channel_id=1, source_target_pairs={{0,4},{1,5},{2,6},{3,7},{4,0},{5,1},{6,2},{7,3},{8,12},{9,13},{10,... | collective-permute-start | bytes 3538952 | tf_op jit(solution)/shard_map/ppermute | solution.py:22
  2.3 57.8 %collective-permute-start = (bf16[512,1152]{1,0:T(8,128)(2,1)}, bf16[512,1152]{1,0:T(8,128)(2,1)S(1)}, u32[]{:S(2)}, u32[]{:S(2)}) collective-permute-start(bf16[512,1152]{1,0:T(8,128)(2,1)} %img_ref.3), channel_id=1, source_target_pairs={{0,128},{8,136},{16,144},{24,152},{32,160},{40,168},{48,176},{56,1... | collective-permute-start | bytes 3538952 | tf_op jit(solution)/shard_map/ppermute | solution.py:22
  8.6 1.8 %copy-start = (bf16[1152,1152]{1,0:T(8,128)(2,1)S(1)}, bf16[1152,1152]{1,0:T(8,128)(2,1)}, u32[]{:S(2)}) copy-start(bf16[1152,1152]{1,0:T(8,128)(2,1)} %head_ref.3) | copy-start | bytes 7962628
  10.4 1.3 copy-start.7
  11.6 18.1 %copy-start.8 = (bf16[512,1152]{1,0:T(8,128)(2,1)S(1)}, bf16[512,1152]{1,0:T(8,128)(2,1)}, u32[]{:S(2)}) copy-start(bf16[512,1152]{1,0:T(8,128)(2,1)} %img_ref.3) | copy-start | bytes 3538948
  11.7 18.1 %copy-start.15 = (s32[1,512]{1,0:T(1,128)S(1)}, s32[1,512]{1,0:T(1,128)}, u32[]{:S(2)}) copy-start(s32[1,512]{1,0:T(1,128)} %across_ref.2) | copy-start | bytes 6148
  17.6 42.5 %copy-start.2 = (bf16[512,1152]{1,0:T(8,128)(2,1)}, bf16[512,1152]{1,0:T(8,128)(2,1)S(1)}, u32[]{:S(2)}) copy-start(bf16[512,1152]{1,0:T(8,128)(2,1)S(1)} %get-tuple-element.26.zt_ref.refs_1_) | copy-start | bytes 3538948
  17.6 24.8 %collective-permute-start.2 = (bf16[256,1152]{1,0:T(8,128)(2,1)}, bf16[256,1152]{1,0:T(8,128)(2,1)S(1)}, u32[]{:S(2)}, u32[]{:S(2)}) collective-permute-start(bf16[256,1152]{1,0:T(8,128)(2,1)} %get-tuple-element.34), channel_id=1, source_target_pairs={{0,4},{1,5},{2,6},{3,7},{4,0},{5,1},{6,2},{7,3},{8,12},{9,13},{10,... | collective-permute-start | bytes 1769480 | tf_op jit(solution)/shard_map/ppermute | solution.py:22
  18.1 35.8 %collective-permute-start.3 = (bf16[256,1152]{1,0:T(8,128)(2,1)}, bf16[256,1152]{1,0:T(8,128)(2,1)S(1)}, u32[]{:S(2)}, u32[]{:S(2)}) collective-permute-start(bf16[256,1152]{1,0:T(8,128)(2,1)} %get-tuple-element.35), channel_id=1, source_target_pairs={{0,4},{1,5},{2,6},{3,7},{4,0},{5,1},{6,2},{7,3},{8,12},{9,13},{10,... | collective-permute-start | bytes 1769480 | tf_op jit(solution)/shard_map/ppermute | solution.py:22
  33.4 1.0 copy-start.10
  53.9 0.8 copy-start.13
  63.7 4.5 %copy-start.5 = (bf16[512,1152]{1,0:T(8,128)(2,1)}, bf16[512,1152]{1,0:T(8,128)(2,1)S(1)}, u32[]{:S(2)}) copy-start(bf16[512,1152]{1,0:T(8,128)(2,1)S(1)} %get-tuple-element.38.du_ref) | copy-start | bytes 3538948
  63.7 3.4 %collective-permute-start.6 = (bf16[1152,640]{1,0:T(8,128)(2,1)S(1)}, bf16[1152,640]{1,0:T(8,128)(2,1)S(1)}, u32[]{:S(2)}, u32[]{:S(2)}) collective-permute-start(bf16[1152,640]{1,0:T(8,128)(2,1)S(1)} %get-tuple-element.37), channel_id=1, source_target_pairs={{0,8},{8,0},{16,24},{24,16},{32,40},{40,32},{48,56},{56,48},{64,72... | collective-permute-start | bytes 4423688 | tf_op jit(solution)/shard_map/ppermute | solution.py:22
  63.8 16.0 %collective-permute-start.4 = (bf16[256,1152]{1,0:T(8,128)(2,1)}, bf16[256,1152]{1,0:T(8,128)(2,1)}, u32[]{:S(2)}, u32[]{:S(2)}) collective-permute-start(bf16[256,1152]{1,0:T(8,128)(2,1)} %get-tuple-element.34), channel_id=1, source_target_pairs={{0,32},{8,40},{16,48},{24,56},{32,64},{40,72},{48,80},{56,88},{64,... | collective-permute-start | bytes 1769480 | tf_op jit(solution)/shard_map/ppermute | solution.py:27
  65.2 15.5 %collective-permute-start.5 = (bf16[256,1152]{1,0:T(8,128)(2,1)}, bf16[256,1152]{1,0:T(8,128)(2,1)}, u32[]{:S(2)}, u32[]{:S(2)}) collective-permute-start(bf16[256,1152]{1,0:T(8,128)(2,1)} %get-tuple-element.35), channel_id=1, source_target_pairs={{0,224},{8,232},{16,240},{24,248},{32,0},{40,8},{48,16},{56,24},{6... | collective-permute-start | bytes 1769480 | tf_op jit(solution)/shard_map/ppermute | solution.py:27
  68.2 1.1 copy-start.4
  69.3 4.6 %copy-start.1 = (bf16[1152,1152]{1,0:T(8,128)(2,1)S(1)}, bf16[1152,1152]{1,0:T(8,128)(2,1)}, u32[]{:S(2)}) copy-start(bf16[1152,1152]{1,0:T(8,128)(2,1)} %head_ref.3) | copy-start | bytes 7962628
  69.3 25.4 %all-to-all-start = ((bf16[8,144,640]{2,1,0:T(8,128)(2,1)}), bf16[8,144,640]{2,1,0:T(8,128)(2,1)}, u32[]{:S(2)}, u32[]{:S(2)}) async-start(bf16[8,144,640]{2,1,0:T(8,128)(2,1)} %bitcast.1), calls=%async_computation | async-start | bytes 2949120 | tf_op jit(solution)/shard_map/all_to_all | solution.py:289
  73.9 1.3 copy-start.6
  78.0 7.9 %copy-start.3 = (bf16[512,1152]{1,0:T(8,128)(2,1)S(1)}, bf16[512,1152]{1,0:T(8,128)(2,1)}, u32[]{:S(2)}) copy-start(bf16[512,1152]{1,0:T(8,128)(2,1)} %copy-done.2) | copy-start | bytes 3538948
  78.0 7.9 %copy-start.11 = (bf16[512,1152]{1,0:T(8,128)(2,1)S(1)}, bf16[512,1152]{1,0:T(8,128)(2,1)}, u32[]{:S(2)}) copy-start(bf16[512,1152]{1,0:T(8,128)(2,1)} %copy-done.10) | copy-start | bytes 3538948
  78.0 7.9 %copy-start.14 = (bf16[256,1152]{1,0:T(8,128)(2,1)S(1)}, bf16[256,1152]{1,0:T(8,128)(2,1)}, u32[]{:S(2)}) copy-start(bf16[256,1152]{1,0:T(8,128)(2,1)} %copy-done.13) | copy-start | bytes 1769476
  80.8 32.6 %collective-permute-start.7 = (bf16[256,1152]{1,0:T(8,128)(2,1)}, bf16[256,1152]{1,0:T(8,128)(2,1)}, u32[]{:S(2)}, u32[]{:S(2)}) collective-permute-start(bf16[256,1152]{1,0:T(8,128)(2,1)} %collective-permute-done.4), channel_id=1, source_target_pairs={{0,64},{8,72},{16,80},{24,88},{32,96},{40,104},{48,112},{56,120},{... | collective-permute-start | bytes 1769480 | tf_op jit(solution)/shard_map/ppermute | solution.py:27
  85.9 29.6 %collective-permute-start.9 = (bf16[256,1152]{1,0:T(8,128)(2,1)}, bf16[256,1152]{1,0:T(8,128)(2,1)}, u32[]{:S(2)}, u32[]{:S(2)}) collective-permute-start(bf16[256,1152]{1,0:T(8,128)(2,1)} %collective-permute-done.5), channel_id=1, source_target_pairs={{0,192},{8,200},{16,208},{24,216},{32,224},{40,232},{48,240},{56,2... | collective-permute-start | bytes 1769480 | tf_op jit(solution)/shard_map/ppermute | solution.py:27
  97.1 22.6 %all-to-all-start.1 = ((bf16[16,48,128]{2,1,0:T(8,128)(2,1)}), bf16[16,48,128]{2,1,0:T(8,128)(2,1)}, u32[]{:S(2)}, u32[]{:S(2)}) async-start(bf16[16,48,128]{2,1,0:T(8,128)(2,1)} %gather.1), calls=%async_computation.1 | async-start | bytes 393216 | tf_op jit(solution)/shard_map/all_to_all | solution.py:318
  106.7 24.0 %copy-start.9 = (bf16[512,1152]{1,0:T(8,128)(2,1)S(1)}, bf16[512,1152]{1,0:T(8,128)(2,1)}, u32[]{:S(2)}) copy-start(bf16[512,1152]{1,0:T(8,128)(2,1)} %img_ref.3) | copy-start | bytes 3538948
  113.4 13.9 %collective-permute-start.8 = (bf16[256,1152]{1,0:T(8,128)(2,1)}, bf16[256,1152]{1,0:T(8,128)(2,1)}, u32[]{:S(2)}, u32[]{:S(2)}) collective-permute-start(bf16[256,1152]{1,0:T(8,128)(2,1)} %collective-permute-done.7), channel_id=1, source_target_pairs={{0,32},{8,40},{16,48},{24,56},{32,64},{40,72},{48,80},{56,88},{64,... | collective-permute-start | bytes 1769480 | tf_op jit(solution)/shard_map/ppermute | solution.py:27
  115.6 15.1 %collective-permute-start.10 = (bf16[256,1152]{1,0:T(8,128)(2,1)}, bf16[256,1152]{1,0:T(8,128)(2,1)}, u32[]{:S(2)}, u32[]{:S(2)}) collective-permute-start(bf16[256,1152]{1,0:T(8,128)(2,1)} %collective-permute-done.9), channel_id=1, source_target_pairs={{0,224},{8,232},{16,240},{24,248},{32,0},{40,8},{48,16},{56,24},{6... | collective-permute-start | bytes 1769480 | tf_op jit(solution)/shard_map/ppermute | solution.py:27
  119.8 10.9 %copy-start.12 = (bf16[512,1152]{1,0:T(8,128)(2,1)S(1)}, bf16[512,1152]{1,0:T(8,128)(2,1)}, u32[]{:S(2)}) copy-start(bf16[512,1152]{1,0:T(8,128)(2,1)} %copy-done.10) | copy-start | bytes 3538948
